TPU v7x, 256 devices: a whole 4x4x8 slice. The times are simulated.
256 devices in a mesh: dp: 16 (over y, x), tensor: 16 (over z, core).
Axes of the slice: x: 4, y: 4, z: 8, core: 2. Of those that a mesh axis runs over, the one named last changes fastest.
Arguments:
- tokens: bfloat16 [4096, 6144], P('dp'), may hold values from -6 to 6
- target: bfloat16 [4096, 6144], P('dp'), may hold values from -6 to 6
- pair_bias: float32 [4096, 32, 256], P('dp', 'tensor'), may hold values from -6 to 680
- neighbours: int32 [4096, 256], P('dp'), may hold values 0 or 1
- w_query: bfloat16 [6144, 4096], P('dp', 'tensor'), may hold values from -0.078125 to 0.078125
- w_key: bfloat16 [6144, 4096], P('dp', 'tensor'), may hold values from -0.078125 to 0.078125
- w_value: bfloat16 [6144, 4096], P('dp', 'tensor'), may hold values from -0.078125 to 0.078125
- w_out: bfloat16 [4096, 6144], P('tensor', 'dp'), may hold values from -0.09375 to 0.09375
- basis_value: float32 [6144, 4096], P('dp', 'tensor'), may hold values from -32 to 32
- basis_out: float32 [4096, 6144], P('tensor', 'dp'), may hold values from -32 to 32
- prior_value: float32 [6144, 4096], P('dp', 'tensor'), may hold values from -32 to 32
- prior_out: float32 [4096, 6144], P('tensor', 'dp'), may hold values from -32 to 32
- prior_beta: float32 [], replicated, may hold values from 10 to 60
Outputs:
- next_value: float32 [6144, 4096], P('dp', 'tensor')
- next_out: float32 [4096, 6144], P('tensor', 'dp')
- coefficients: float32 [2], replicated
All inputs are finite; a program needn't handle non-finite values. No bound on the sum of `neighbours` on one device may be relied on, other than what follows from the above.
Results may differ from a plain program's by a relative error of at most 0.02.
Values may be sent and summed in bfloat16 or wider, within the bound.
A program may use at most 128 MiB of HBM per device.

v0:
```python
import math

import jax
import jax.numpy as jnp
from jax import lax
from jax.sharding import PartitionSpec as P

HEAD_DIM = 128


loss_gain = 32.0
epsilon = 1e-06


def body(
    tokens,
    target,
    pair_bias,
    neighbours,
    w_query,
    w_key,
    w_value,
    w_out,
    basis_value,
    basis_out,
    prior_value,
    prior_out,
    prior_beta,
):
    count = tokens.shape[0]
    features = tokens.shape[1]
    local_width = w_query.shape[1]
    heads_here = local_width // HEAD_DIM
    full_width = local_width * lax.axis_size("tensor")
    groups = lax.axis_size("dp")
    total_tokens = count * groups
    xf = tokens.astype(jnp.float32)
    normed = (xf * lax.rsqrt(jnp.mean(xf * xf, axis=1, keepdims=True) + epsilon)).astype(
        jnp.bfloat16
    )
    basis_value_b = basis_value.astype(jnp.bfloat16)
    pieces = (
        lax.all_gather(w_query, "dp", axis=0, tiled=True),
        lax.all_gather(w_key, "dp", axis=0, tiled=True),
        lax.all_gather(w_value, "dp", axis=0, tiled=True),
        lax.all_gather(basis_value_b, "dp", axis=0, tiled=True),
    )
    query_acc, key_acc, value_acc, tangent_acc = tuple(
        (jnp.dot(normed, piece, preferred_element_type=jnp.float32) for piece in pieces)
    )
    shape3 = (count, heads_here, HEAD_DIM)
    query = query_acc.astype(jnp.bfloat16).reshape(shape3)
    keys = key_acc.astype(jnp.bfloat16).reshape(shape3)
    values = value_acc.astype(jnp.bfloat16).reshape(shape3)
    tangent_values = (tangent_acc / math.sqrt(features)).astype(jnp.bfloat16).reshape(shape3)
    out_full, tangent_out = (
        lax.all_gather(w_out, "dp", axis=1, tiled=True),
        lax.all_gather(basis_out.astype(jnp.bfloat16), "dp", axis=1, tiled=True),
    )
    scores = (
        jnp.einsum("thd,shd->ths", query, keys, preferred_element_type=jnp.float32)
        / math.sqrt(HEAD_DIM)
        + pair_bias
    )
    rows = lax.broadcasted_iota(jnp.int32, (count, count), 0)
    cols = lax.broadcasted_iota(jnp.int32, (count, count), 1)
    allowed = (neighbours == 1) | (jnp.abs(rows - cols) <= 1)
    scores = jnp.where(allowed[:, None, :], scores, -jnp.inf)
    probs = jax.nn.softmax(scores, axis=2).astype(jnp.bfloat16)
    mixed = (
        jnp.einsum("ths,shd->thd", probs, values, preferred_element_type=jnp.float32)
        .astype(jnp.bfloat16)
        .reshape(count, local_width)
    )
    tangent_mixed = (
        jnp.einsum("ths,shd->thd", probs, tangent_values, preferred_element_type=jnp.float32)
        .astype(jnp.bfloat16)
        .reshape(count, local_width)
    )
    scale_out = 1.0 / math.sqrt(full_width)
    partial_value = jnp.dot(mixed, out_full, preferred_element_type=jnp.float32)
    tangent_partial = jnp.dot(
        mixed, tangent_out, preferred_element_type=jnp.float32
    ) * scale_out + jnp.dot(tangent_mixed, out_full, preferred_element_type=jnp.float32)
    attn, tangent_attn = (
        lax.psum(partial_value.astype(jnp.bfloat16), "tensor").astype(jnp.float32),
        lax.psum(tangent_partial.astype(jnp.bfloat16), "tensor").astype(jnp.float32),
    )
    factor = loss_gain * full_width / total_tokens
    error = ((xf + attn - target.astype(jnp.float32)) * factor).astype(jnp.bfloat16)
    tangent_error = (tangent_attn * factor).astype(jnp.bfloat16)
    first = jnp.einsum("td,ta->da", error, tangent_mixed, preferred_element_type=jnp.float32)
    second = jnp.einsum("td,ta->da", tangent_error, mixed, preferred_element_type=jnp.float32)
    curv_out = (
        lax.psum_scatter(
            ((first + second) * scale_out).astype(jnp.bfloat16),
            "dp",
            scatter_dimension=0,
            tiled=True,
        )
        .astype(jnp.float32)
        .T
    )
    back_tangent = (
        jnp.einsum("td,ad->ta", tangent_error, out_full, preferred_element_type=jnp.float32)
        + jnp.einsum("td,ad->ta", error, tangent_out, preferred_element_type=jnp.float32)
        * scale_out
    ).astype(jnp.bfloat16)
    value_back = (
        jnp.einsum(
            "ths,thd->shd", probs, back_tangent.reshape(shape3), preferred_element_type=jnp.float32
        )
        .astype(jnp.bfloat16)
        .reshape(count, local_width)
    )
    scale_value = 1.0 / math.sqrt(features)
    curv_value = lax.psum_scatter(
        (
            jnp.einsum("ti,ta->ia", normed, value_back, preferred_element_type=jnp.float32)
            * scale_value
        ).astype(jnp.bfloat16),
        "dp",
        scatter_dimension=0,
        tiled=True,
    ).astype(jnp.float32)
    entries = 2.0 * features * full_width
    alpha = (
        lax.psum(
            jnp.sum(basis_value * curv_value) + jnp.sum(basis_out * curv_out), ("dp", "tensor")
        )
        / entries
    )
    rest_value = curv_value - alpha * basis_value - prior_beta * prior_value
    rest_out = curv_out - alpha * basis_out - prior_beta * prior_out
    squares = (
        lax.psum(jnp.sum(rest_value * rest_value) + jnp.sum(rest_out * rest_out), ("dp", "tensor"))
        / entries
    )
    beta = jnp.sqrt(squares + epsilon)
    return (rest_value / beta, rest_out / beta, jnp.stack([alpha, beta]))


def solution(mesh):
    placed = (
        P("dp", None),
        P("dp", None),
        P("dp", "tensor", None),
        P("dp", None),
        P("dp", "tensor"),
        P("dp", "tensor"),
        P("dp", "tensor"),
        P("tensor", "dp"),
        P("dp", "tensor"),
        P("tensor", "dp"),
        P("dp", "tensor"),
        P("tensor", "dp"),
        P(),
    )
    return jax.shard_map(
        body,
        mesh=mesh,
        in_specs=placed,
        out_specs=(P("dp", "tensor"), P("tensor", "dp"), P()),
        check_vma=False,
    )
```

profile of v0, /device:TPU:1, one launch (start us, length us, event | category | flops | bytes accessed | tf_op | source)
XLA Modules:
  0.0 824.5 jit_solution(4294563663317649409)
XLA Ops:
  7.2 0.7 all-gather.9.cloned.1.call-update
  8.0 0.7 all-gather.11.cloned.1.call-update
  8.7 0.7 all-gather.7.cloned.1.call-update
  9.4 1.7 convert_element_type.88
  11.2 0.5 all-gather.17.cloned.1.call-update
  11.8 1.7 convert_element_type.87
  13.6 2.1 copy.19
  15.7 0.2 copy.16
  15.9 0.7 fusion.5
  16.6 50.3 %all-gather.9.cloned.1.call-done = bf16[6144,256]{1,0:T(8,128)(2,1)} async-done(((bf16[384,256]{1,0:T(8,128)(2,1)}), bf16[6144,256]{1,0:T(8,128)(2,1)}) %all-gather.9.cloned.1.call-update) | async-done | bytes 3145744 | tf_op jit(solution)/shard_map/all_gather | solution.py:44
  66.9 3.4 convolution_convert_fusion.5
  70.4 51.0 %all-gather.11.cloned.1.call-done = bf16[6144,256]{1,0:T(8,128)(2,1)} async-done(((bf16[384,256]{1,0:T(8,128)(2,1)}), bf16[6144,256]{1,0:T(8,128)(2,1)}) %all-gather.11.cloned.1.call-update) | async-done | bytes 3145744 | tf_op jit(solution)/shard_map/all_gather | solution.py:43
  121.3 3.4 convolution_convert_fusion.4
  124.8 2.2 fusion.34
  127.0 1.1 divide_convert_fusion
  128.1 47.7 %all-gather.7.cloned.1.call-done = bf16[6144,256]{1,0:T(8,128)(2,1)} async-done(((bf16[384,256]{1,0:T(8,128)(2,1)}), bf16[6144,256]{1,0:T(8,128)(2,1)}) %all-gather.7.cloned.1.call-update) | async-done | bytes 3145744 | tf_op jit(solution)/shard_map/all_gather | solution.py:45
  175.8 3.4 convolution_convert_fusion.6
  179.2 0.2 convolution_convert_fusion.3
  179.4 51.2 %all-gather.15.cloned.1.call-done = bf16[6144,256]{1,0:T(8,128)(2,1)} async-done(((bf16[384,256]{1,0:T(8,128)(2,1)}), bf16[6144,256]{1,0:T(8,128)(2,1)}) %all-gather.15.cloned.1.call-update) | async-done | bytes 3145744 | tf_op jit(solution)/shard_map/all_gather | solution.py:46
  230.6 3.4 fusion.18
  234.0 0.8 convolution_convert_fusion.2
  234.9 54.0 %all-gather.17.cloned.1.call-done = bf16[256,6144]{1,0:T(8,128)(2,1)} async-done(((bf16[256,384]{1,0:T(8,128)(2,1)}), bf16[256,6144]{1,0:T(8,128)(2,1)}) %all-gather.17.cloned.1.call-update) | async-done | bytes 3145744 | tf_op jit(solution)/shard_map/all_gather | solution.py:57
  288.9 4.5 convolution_convert_fusion
  293.4 55.4 %all-gather.13.cloned.1.call-done = bf16[256,6144]{1,0:T(8,128)(2,1)} async-done(((bf16[256,384]{1,0:T(8,128)(2,1)}), bf16[256,6144]{1,0:T(8,128)(2,1)}) %all-gather.13.cloned.1.call-update) | async-done | bytes 3145744 | tf_op jit(solution)/shard_map/all_gather | solution.py:58
  348.8 3.0 convolution_multiply_fusion.1
  351.9 2.7 fusion.3
  354.6 0.2 reduce-scatter.3.cloned.1.call-start
  354.8 127.6 %all-reduce.3.cloned.1.call-done = (bf16[256,6144]{1,0:T(8,128)(2,1)}, bf16[256,6144]{1,0:T(8,128)(2,1)}) async-done(((bf16[256,6144]{1,0:T(8,128)(2,1)}, bf16[256,6144]{1,0:T(8,128)(2,1)}), (bf16[256,6144]{1,0:T(8,128)(2,1)}, bf16[256,6144]{1,0:T(8,128)(2,1)})) %all-reduce.3.cloned.1.call-update) | async-done | bytes 6291472 | tf_op jit(solution)/shard_map/psum | solution.py:86
  482.4 5.5 convolution_multiply_fusion.3
  488.0 1.0 fusion.17
  489.0 0.2 convolution_convert_fusion.1
  489.2 3.0 fusion.4
  492.3 0.8 copy-done.11
  493.1 5.5 fusion.26
  498.6 3.3 fusion.2
  501.9 1.0 copy-done.8
  503.7 68.5 %reduce-scatter.3.cloned.1.call-done = bf16[384,256]{1,0:T(8,128)(2,1)} async-done(((bf16[6144,256]{1,0:T(8,128)(2,1)}), bf16[384,256]{1,0:T(8,128)(2,1)}) %reduce-scatter.3.cloned.1.call-update) | async-done | bytes 196624 | tf_op jit(solution)/shard_map/reduce_scatter | solution.py:117
  572.2 1.7 fusion.19
  573.9 82.0 %reduce-scatter.5.cloned.1.call-done = bf16[384,256]{1,0:T(8,128)(2,1)} async-done(((bf16[6144,256]{1,0:T(8,128)(2,1)}), bf16[384,256]{1,0:T(8,128)(2,1)}) %reduce-scatter.5.cloned.1.call-update) | async-done | bytes 196624 | tf_op jit(solution)/shard_map/reduce_scatter | solution.py:95
  655.9 1.7 fusion.21
  658.9 0.2 copy.25
  659.1 77.2 %psum.30 = f32[]{:T(128)} all-reduce(f32[]{:T(128)S(6)} %add.54), channel_id=1, replica_groups=mesh['dp'=16,'tensor'=16] {'dp','tensor'}, use_global_device_ids=true, to_apply=%region_9.10 | all-reduce | flops 1 | bytes 8 | tf_op jit(solution)/shard_map/psum | solution.py:128
  736.9 1.6 multiply_reduce_fusion.1
  738.6 1.6 multiply_reduce_fusion
  741.5 73.3 %psum.31 = f32[]{:T(128)} all-reduce(f32[]{:T(128)S(6)} %add.55), channel_id=1, replica_groups=mesh['dp'=16,'tensor'=16] {'dp','tensor'}, use_global_device_ids=true, to_apply=%region_12.13 | all-reduce | flops 1 | bytes 8 | tf_op jit(solution)/shard_map/psum | solution.py:136
  815.6 0.9 copy.26
  816.5 0.6 pad_maximum_fusion
  817.1 0.8 broadcast_divide_fusion.1
  (43 shorter events, 0.8 us)
Async XLA Ops:
  7.2 8.5 %copy-start.13 = (s32[256,256]{1,0:T(8,128)S(1)}, s32[256,256]{1,0:T(8,128)}, u32[]{:S(2)}) copy-start(s32[256,256]{1,0:T(8,128)} %param.16) | copy-start | bytes 786436
  7.2 8.7 %copy-start = (bf16[256,6144]{1,0:T(8,128)(2,1)S(1)}, bf16[256,6144]{1,0:T(8,128)(2,1)}, u32[]{:S(2)}) copy-start(bf16[256,6144]{1,0:T(8,128)(2,1)} %param.13) | copy-start | bytes 9437188
  7.2 59.8 %all-gather.9.cloned.1.call-start = ((), (), s32[]{:S(2)}) async-start(), calls=%async_computation.3 | async-start | bytes 3342336 | tf_op jit(solution)/shard_map/all_gather | solution.py:44
  7.9 113.4 %all-gather.11.cloned.1.call-start = ((), (), s32[]{:S(2)}) async-start(), calls=%async_computation.4 | async-start | bytes 3342336 | tf_op jit(solution)/shard_map/all_gather | solution.py:43
  8.7 167.1 %all-gather.7.cloned.1.call-start = ((), (), s32[]{:S(2)}) async-start(), calls=%async_computation.2 | async-start | bytes 3342336 | tf_op jit(solution)/shard_map/all_gather | solution.py:45
  9.4 221.2 %all-gather.15.cloned.1.call-start = ((), (), s32[]{:S(2)}) async-start(), calls=%async_computation.6 | async-start | bytes 3342336 | tf_op jit(solution)/shard_map/all_gather | solution.py:46
  11.2 277.7 %all-gather.17.cloned.1.call-start = ((), (), s32[]{:S(2)}) async-start(), calls=%async_computation.7 | async-start | bytes 3342336 | tf_op jit(solution)/shard_map/all_gather | solution.py:57
  11.8 337.0 %all-gather.13.cloned.1.call-start = ((), (), s32[]{:S(2)}) async-start(), calls=%async_computation.5 | async-start | bytes 3342336 | tf_op jit(solution)/shard_map/all_gather | solution.py:58
  13.5 468.8 %all-reduce.3.cloned.1.call-start = ((), (), s32[]{:S(2)}) async-start(), calls=%async_computation.10 | async-start | bytes 12582912 | tf_op jit(solution)/shard_map/psum | solution.py:86
  348.8 3.1 copy-start.1
  348.8 3.1 copy-start.10
  354.6 217.6 %reduce-scatter.3.cloned.1.call-start = ((), (), s32[]{:S(2)}) async-start(), calls=%async_computation.8 | async-start | bytes 3342336 | tf_op jit(solution)/shard_map/reduce_scatter | solution.py:117
  482.4 5.5 copy-start.2
  482.4 5.6 copy-start.4
  492.2 0.9 copy-start.11
  492.2 163.7 %reduce-scatter.5.cloned.1.call-start = ((), (), s32[]{:S(2)}) async-start(), calls=%async_computation.9 | async-start | bytes 3342336 | tf_op jit(solution)/shard_map/reduce_scatter | solution.py:95
  493.1 5.5 copy-start.5
  501.9 1.0 copy-start.8
  501.9 70.3 %copy-start.3 = (f32[384,256]{1,0:T(8,128)S(1)}, f32[384,256]{1,0:T(8,128)}, u32[]{:S(2)}) copy-start(f32[384,256]{1,0:T(8,128)} %param.21) | copy-start | bytes 1179652
  501.9 157.0 %copy-start.12 = (f32[256,384]{1,0:T(8,128)S(1)}, f32[256,384]{1,0:T(8,128)}, u32[]{:S(2)}) copy-start(f32[256,384]{1,0:T(8,128)} %param.24) | copy-start | bytes 1179652
  501.9 235.1 %copy-start.9 = (f32[384,256]{1,0:T(8,128)S(1)}, f32[384,256]{1,0:T(8,128)}, u32[]{:S(2)}) copy-start(f32[384,256]{1,0:T(8,128)} %param.23) | copy-start | bytes 1179652
  572.2 245.0 %copy-start.6 = (bf16[384,256]{1,0:T(8,128)(2,1)S(1)}, bf16[384,256]{1,0:T(8,128)(2,1)}, u32[]{:S(2)}) copy-start(bf16[384,256]{1,0:T(8,128)(2,1)} %reduce-scatter.3.cloned.1.call-done) | copy-start | bytes 589828
  655.9 159.6 %copy-start.7 = (bf16[384,256]{1,0:T(8,128)(2,1)S(1)}, bf16[384,256]{1,0:T(8,128)(2,1)}, u32[]{:S(2)}) copy-start(bf16[384,256]{1,0:T(8,128)(2,1)} %reduce-scatter.5.cloned.1.call-done) | copy-start | bytes 589828
Sparse Core Ops, SparseCore 0:
  10.4 56.4 all-gather.8
  69.4 51.9 all-gather.10
  123.8 51.9 all-gather.6
  178.6 51.9 all-gather.14
  232.8 56.0 all-gather.16
  291.7 57.0 all-gather.12
  354.7 127.6 all-reduce.2
  492.3 79.7 reduce-scatter.2
  575.8 80.0 reduce-scatter.4
where the time goes:
time: 825 us; the launch traced here: 824 us
  waiting for transfers between devices  590 us (72%)
  blocking collectives  150 us (18%)
  matrix products  45.7 us (6%)
  between operations  18.6 us (2%)
  other arithmetic  13.4 us (2%)
    psum x1, waiting for transfers between devices, body(): lax.psum(partial_value.astype(jnp.bfloat16), 'tensor').astype(jnp.float32)  128 us
    reduce_scatter x1, waiting for transfers between devices, body(): lax.psum_scatter(((first + second) * scale_out).astype(jnp.bfloat16), 'dp...  82 us
    psum x1, blocking collectives, body(): lax.psum(jnp.sum(basis_value * curv_value) + jnp.sum(basis_out * curv_out...  77.2 us
    psum x1, blocking collectives, body(): lax.psum(jnp.sum(rest_value * rest_value) + jnp.sum(rest_out * rest_out),...  73.3 us
    reduce_scatter x1, waiting for transfers between devices, body(): lax.psum_scatter((jnp.einsum('ti,ta->ia', normed, value_back, preferred_e...  68.5 us
    all_gather x1, waiting for transfers between devices, body(): lax.all_gather(basis_out.astype(jnp.bfloat16), 'dp', axis=1, tiled=True)  55.4 us
    all_gather x1, waiting for transfers between devices, body(): lax.all_gather(w_out, 'dp', axis=1, tiled=True)  54 us
    all_gather x1, waiting for transfers between devices, body(): lax.all_gather(basis_value_b, 'dp', axis=0, tiled=True)  51.2 us
  transfers between devices with their start and end apart: 9, of which 9 were waited for; matrix products, arithmetic and copies ran while one was open for 5% of the time, Pallas kernels for 0%

commit v1 on v0

v1 whole, which is shorter than its diff:
```python
import math

import jax
import jax.numpy as jnp
from jax import lax
from jax.experimental import pallas as pl
from jax.experimental.pallas import tpu as pltpu
from jax.sharding import PartitionSpec as P

HEAD_DIM = 128
SIDE = 4
ROWS = 16

loss_gain = 32.0
epsilon = 1e-06

MESH = pl.DeviceIdType.MESH
BF = jnp.bfloat16
F32 = jnp.float32
VMEM = pl.BlockSpec(memory_space=pltpu.VMEM)
SMEM = pl.BlockSpec(memory_space=pltpu.SMEM)
DMA = pltpu.SemaphoreType.DMA


def coords():
    dp = lax.axis_index("dp")
    t = lax.axis_index("tensor")
    return dp // SIDE, dp % SIDE, t


def at(y, x, t):
    return (((y + 2 * SIDE) % SIDE) * SIDE + (x + 2 * SIDE) % SIDE, (t + 32) % 16)


def along_x(j):
    y, x, t = coords()
    return at(y, x + j, t)


def along_y(j):
    y, x, t = coords()
    return at(y + j, x, t)


def along_t(k):
    y, x, t = coords()
    return at(y, x, t + k)


def along_z(k):
    y, x, t = coords()
    return at(y, x, t + 2 * k)


def other_core():
    y, x, t = coords()
    return at(y, x, t + 1 - 2 * (t % 2))


def greet(peers):
    barrier = pltpu.get_barrier_semaphore()
    for peer in peers:
        pl.semaphore_signal(barrier, inc=1, device_id=peer, device_id_type=MESH)
    pl.semaphore_wait(barrier, len(peers))


def send(src, dst, ssem, rsem, peer):
    copy = pltpu.make_async_remote_copy(
        src_ref=src,
        dst_ref=dst,
        send_sem=ssem,
        recv_sem=rsem,
        device_id=peer,
        device_id_type=MESH,
    )
    copy.start()
    return copy


def call(kernel, number, out_shape, scratch, *args, in_specs=None):
    return pl.pallas_call(
        kernel,
        out_shape=out_shape,
        in_specs=in_specs or [VMEM] * len(args),
        out_specs=jax.tree.map(lambda _: VMEM, out_shape),
        scratch_shapes=scratch,
        compiler_params=pltpu.CompilerParams(
            collective_id=number, has_side_effects=True, vmem_limit_bytes=48 * 2**20
        ),
    )(*args)


def shape(dims, dtype):
    return jax.ShapeDtypeStruct(dims, dtype)


NEAR = (1, 3, 2)


def spread_kernel(piece, wqk, wvt, diff, rows, gqk, gvt, diffs, ps, pr, ws, wr, ds, dr, zs, zr, cs, cr, ls):
    y, x, t = coords()
    peers = [along_x(j) for j in NEAR] + [along_y(j) for j in NEAR]
    corners = [at(y + i, x + j, t) for i in NEAR for j in NEAR]
    greet(peers + corners + [along_z(1), along_z(-1), other_core()])
    copies = []
    pieces = []
    for j in NEAR:
        pieces.append(
            send(piece.at[j - 1], rows.at[j - 1, t], ps.at[j - 1], pr.at[j - 1], along_x(j))
        )
        pieces.append(
            send(piece.at[j + 2], rows.at[j + 2, t], ps.at[j + 2], pr.at[j + 2], along_y(j))
        )
    for j in NEAR:
        copies.append(send(wqk, gqk.at[y], ws.at[j - 1], wr.at[j - 1], along_y(j)))
        copies.append(send(wvt, gvt.at[x], ws.at[j + 2], wr.at[j + 2], along_x(j)))
    me = y * SIDE + x
    k = 0
    for i in range(SIDE):
        for j in range(SIDE):
            if i or j:
                yy, xx = (y + i) % SIDE, (x + j) % SIDE
                copies.append(
                    send(
                        diff.at[yy * SIDE + xx],
                        diffs.at[me],
                        ds.at[k],
                        dr.at[k],
                        (yy * SIDE + xx, t),
                    )
                )
                k += 1
    mine = [
        pltpu.make_async_copy(wqk, gqk.at[y], ls.at[0]),
        pltpu.make_async_copy(wvt, gvt.at[x], ls.at[1]),
        pltpu.make_async_copy(diff.at[me], diffs.at[me], ls.at[2]),
    ]
    for copy in mine:
        copy.start()
    for copy in pieces:
        copy.wait_recv()
    c = t % 2
    own = rows.at[:, t]
    copies.append(send(own, own, zs.at[0, 0], zr.at[0, 0], along_z(1)))
    copies.append(send(own, own, zs.at[1, 0], zr.at[1, 0], along_z(-1)))
    copies.append(send(own, own, cs.at[0], cr.at[0], other_core()))
    for step in range(1, 4):
        for way in range(2):
            sign = 1 - 2 * way
            slot = (t - 2 * sign * step + 32) % 16
            got = rows.at[:, slot]
            arrived = pltpu.make_async_remote_copy(
                src_ref=got,
                dst_ref=got,
                send_sem=zs.at[way, step - 1],
                recv_sem=zr.at[way, step - 1],
                device_id=along_z(-sign),
                device_id_type=MESH,
            )
            arrived.wait_recv()
            part = got if step < 3 else rows.at[pl.ds(3 * way, 3), slot]
            copies.append(send(part, part, zs.at[way, step], zr.at[way, step], along_z(sign)))
            k = 2 * step - 1 + way
            copies.append(send(got, got, cs.at[k], cr.at[k], other_core()))
    far = (t + 8) % 16
    for way in range(2):
        part = rows.at[pl.ds(3 * way, 3), far]
        pltpu.make_async_remote_copy(
            src_ref=part,
            dst_ref=part,
            send_sem=zs.at[way, 3],
            recv_sem=zr.at[way, 3],
            device_id=along_z(1),
            device_id_type=MESH,
        ).wait_recv()
    far_ref = rows.at[:, far]
    copies.append(send(far_ref, far_ref, cs.at[7], cr.at[7], other_core()))
    for copy in pieces:
        copy.wait_send()
    for copy in mine:
        copy.wait()
    for copy in copies[:21]:
        copy.wait()
    for copy in copies[21:]:
        copy.wait_send()
    for k in range(8):
        step, way = (k + 1) // 2, (k + 1) % 2
        shift = 8 if k == 7 else 2 * step * (1 - 2 * way)
        slot = (t + 1 - 2 * c - shift + 32) % 16
        got = rows.at[:, slot]
        pltpu.make_async_remote_copy(
            src_ref=got,
            dst_ref=got,
            send_sem=cs.at[k],
            recv_sem=cr.at[k],
            device_id=other_core(),
            device_id_type=MESH,
        ).wait_recv()


def spread(piece, wqk, wvt, diff):
    wide = piece.shape[2]
    return call(
        spread_kernel,
        0,
        (
            shape((6, 16, ROWS, wide), BF),
            shape((SIDE,) + wqk.shape, BF),
            shape((SIDE,) + wvt.shape, BF),
            shape(diff.shape, F32),
        ),
        [
            DMA((6,)),
            DMA((6,)),
            DMA((6,)),
            DMA((6,)),
            DMA((15,)),
            DMA((15,)),
            DMA((2, 4)),
            DMA((2, 4)),
            DMA((8,)),
            DMA((8,)),
            DMA((3,)),
        ],
        piece,
        wqk,
        wvt,
        diff,
    )


def swap_kernel(sign, whole, a, b, ra, rb, ss, rs):
    greet([along_x(j) for j in NEAR] + [along_y(j) for j in NEAR])
    copies = []
    for j in NEAR:
        src = a if whole else a.at[j - 1]
        copies.append(send(src, ra.at[j - 1], ss.at[j - 1], rs.at[j - 1], along_x(sign * j)))
        src = b if whole else b.at[j - 1]
        copies.append(send(src, rb.at[j - 1], ss.at[j + 2], rs.at[j + 2], along_y(sign * j)))
    for copy in copies:
        copy.wait()


def swap(number, sign, whole, a, b):
    def kernel(*refs):
        swap_kernel(sign, whole, *refs)

    lead = (3,) if whole else ()
    return call(
        kernel,
        number,
        (shape(lead + a.shape, a.dtype), shape(lead + b.shape, b.dtype)),
        [DMA((6,)), DMA((6,))],
        a,
        b,
    )


def mix_kernel(mix, full, ts, tr, as_, ar, bs, br, ls):
    y, x, t = coords()
    greet(
        [along_t(k) for k in range(1, 16)]
        + [along_x(j) for j in NEAR]
        + [along_y(j) for j in NEAR]
    )
    copies = []
    for k in range(1, 16):
        to = (t + k) % 16
        copies.append(
            send(
                mix.at[pl.ds(pl.multiple_of(to * ROWS, ROWS), ROWS)],
                full.at[y, x, t],
                ts.at[k],
                tr.at[k],
                along_t(k),
            )
        )
    own = pltpu.make_async_copy(
        mix.at[pl.ds(pl.multiple_of(t * ROWS, ROWS), ROWS)], full.at[y, x, t], ls.at[0]
    )
    own.start()
    own.wait()
    for copy in copies:
        copy.wait_recv()
    low, high = pl.ds(0, 8), pl.ds(8, 8)
    first, second = [], []
    a, b = full.at[y, x, low], full.at[y, x, high]
    for j in NEAR:
        first.append(send(a, a, as_.at[0, j - 1], ar.at[0, j - 1], along_x(j)))
        first.append(send(b, b, bs.at[0, j - 1], br.at[0, j - 1], along_y(j)))
    for j in NEAR:
        second.append(send(a, a, as_.at[1, j - 1], ar.at[1, j - 1], along_y(j)))
        second.append(send(b, b, bs.at[1, j - 1], br.at[1, j - 1], along_x(j)))
    for i in NEAR:
        k = NEAR.index(i) * 2
        first[k].wait_recv()
        first[k + 1].wait_recv()
        a = full.at[y, (x - i + SIDE) % SIDE, low]
        b = full.at[(y - i + SIDE) % SIDE, x, high]
        for j in NEAR:
            second.append(send(a, a, as_.at[1 + i, j - 1], ar.at[1 + i, j - 1], along_y(j)))
            second.append(send(b, b, bs.at[1 + i, j - 1], br.at[1 + i, j - 1], along_x(j)))
    for copy in second:
        copy.wait()
    for copy in first + copies:
        copy.wait_send()


def spread_mix(mix):
    return call(
        mix_kernel,
        1,
        shape((SIDE, SIDE, 16, ROWS, mix.shape[1]), BF),
        [DMA((16,)), DMA((16,)), DMA((5, 3)), DMA((5, 3)), DMA((5, 3)), DMA((5, 3)), DMA((1,))],
        mix,
    )


def back_kernel(part, out, ra, rb, sa, sb, qa, qb, done, s1, r1, s2, r2, ts, tr, ls):
    y, x, t = coords()
    half = part.shape[3] // 2
    low, high = pl.ds(0, half), pl.ds(half, half)
    greet(
        [along_t(k) for k in range(1, 16)]
        + [along_x(j) for j in NEAR]
        + [along_y(j) for j in NEAR]
    )
    first, second, third = [], [], []
    for j in NEAR:
        first.append(
            send(part.at[(y + j) % SIDE, :, :, low], ra.at[j - 1], s1.at[0, j - 1], r1.at[0, j - 1], along_y(j))
        )
        first.append(
            send(part.at[:, (x + j) % SIDE, :, high], rb.at[j - 1], s1.at[1, j - 1], r1.at[1, j - 1], along_x(j))
        )
    for copy in first:
        copy.wait_recv()
    for i in range(SIDE):
        total = part[y, i, :, :half].astype(F32)
        for j in range(3):
            total = total + ra[j, i].astype(F32)
        sa[i] = total.astype(BF)
        total = part[i, x, :, half:].astype(F32)
        for j in range(3):
            total = total + rb[j, i].astype(F32)
        sb[i] = total.astype(BF)
    for j in NEAR:
        second.append(send(sa.at[(x + j) % SIDE], qa.at[j - 1], s2.at[0, j - 1], r2.at[0, j - 1], along_x(j)))
        second.append(send(sb.at[(y + j) % SIDE], qb.at[j - 1], s2.at[1, j - 1], r2.at[1, j - 1], along_y(j)))
    for copy in second:
        copy.wait_recv()
    total = sa[x].astype(F32)
    for j in range(3):
        total = total + qa[j].astype(F32)
    wide = out.shape[2]
    for k in range(8):
        done[k] = total[:, k * wide : (k + 1) * wide].astype(BF)
    total = sb[y].astype(F32)
    for j in range(3):
        total = total + qb[j].astype(F32)
    for k in range(8):
        done[8 + k] = total[:, k * wide : (k + 1) * wide].astype(BF)
    for k in range(1, 16):
        third.append(send(done.at[(t + k) % 16], out.at[t], ts.at[k], tr.at[k], along_t(k)))
    own = pltpu.make_async_copy(done.at[t], out.at[t], ls.at[0])
    own.start()
    own.wait()
    for copy in third:
        copy.wait()
    for copy in first + second:
        copy.wait_send()


def collect_back(part):
    half = part.shape[3] // 2
    return call(
        back_kernel,
        2,
        shape((16, ROWS, part.shape[3] // 16), BF),
        [
            pltpu.VMEM((3, SIDE, ROWS, half), BF),
            pltpu.VMEM((3, SIDE, ROWS, half), BF),
            pltpu.VMEM((SIDE, ROWS, half), BF),
            pltpu.VMEM((SIDE, ROWS, half), BF),
            pltpu.VMEM((3, ROWS, half), BF),
            pltpu.VMEM((3, ROWS, half), BF),
            pltpu.VMEM((16, ROWS, part.shape[3] // 16), BF),
            DMA((2, 3)),
            DMA((2, 3)),
            DMA((2, 3)),
            DMA((2, 3)),
            DMA((16,)),
            DMA((16,)),
            DMA((1,)),
        ],
        part,
    )


def last_kernel(
    entries, cv, co, bv, bo, pv, po, pb, nv, no, coef, one, two, s1, r1, s2, r2
):
    y, x, t = coords()
    me = y * SIDE + x
    greet(
        [along_t(k) for k in range(1, 16)]
        + [at(y + i, x + j, t) for i in range(SIDE) for j in range(SIDE) if i or j]
    )

    def total(value, turn):
        one[turn, t] = jnp.full((8, 128), value, F32)
        copies = []
        for k in range(1, 16):
            copies.append(
                send(one.at[turn, t], one.at[turn, t], s1.at[turn, k], r1.at[turn, k], along_t(k))
            )
        for copy in copies:
            copy.wait()
        two[turn, me] = jnp.sum(one[turn], axis=0)
        copies = []
        k = 0
        for i in range(SIDE):
            for j in range(SIDE):
                if i or j:
                    copies.append(
                        send(
                            two.at[turn, me],
                            two.at[turn, me],
                            s2.at[turn, k],
                            r2.at[turn, k],
                            at(y + i, x + j, t),
                        )
                    )
                    k += 1
        for copy in copies:
            copy.wait()
        return jnp.sum(two[turn], axis=0)[0:1, 0:1] / entries

    alpha = total(jnp.sum(bv[...] * cv[...]) + jnp.sum(bo[...] * co[...]), 0)
    nv[...] = cv[...] - alpha * bv[...] - pb[0, 0] * pv[...]
    no[...] = co[...] - alpha * bo[...] - pb[0, 0] * po[...]
    squares = total(jnp.sum(nv[...] * nv[...]) + jnp.sum(no[...] * no[...]), 1)
    beta = jnp.sqrt(squares + epsilon)
    nv[...] = nv[...] / beta
    no[...] = no[...] / beta
    coef[0:1] = jnp.broadcast_to(alpha, (1, 128))
    coef[1:2] = jnp.broadcast_to(beta, (1, 128))


def finish(entries, cv, co, bv, bo, pv, po, pb):
    def kernel(*refs):
        last_kernel(entries, *refs)

    nv, no, coef = call(
        kernel,
        3,
        (shape(cv.shape, F32), shape(co.shape, F32), shape((8, 128), F32)),
        [
            pltpu.VMEM((2, 16, 8, 128), F32),
            pltpu.VMEM((2, 16, 8, 128), F32),
            DMA((2, 16)),
            DMA((2, 16)),
            DMA((2, 15)),
            DMA((2, 15)),
        ],
        cv,
        co,
        bv,
        bo,
        pv,
        po,
        pb.reshape(1, 1),
        in_specs=[VMEM] * 6 + [SMEM],
    )
    return nv, no, coef[:2, 0]


def pick(array, index, axis):
    return lax.dynamic_index_in_dim(array, index, axis, keepdims=False)


def body(
    tokens,
    target,
    pair_bias,
    neighbours,
    w_query,
    w_key,
    w_value,
    w_out,
    basis_value,
    basis_out,
    prior_value,
    prior_out,
    prior_beta,
):
    count, features = tokens.shape
    local_width = w_query.shape[1]
    heads_here = local_width // HEAD_DIM
    full_width = local_width * lax.axis_size("tensor")
    groups = lax.axis_size("dp")
    total_tokens = count * groups
    block = features // groups
    dp = lax.axis_index("dp")
    t = lax.axis_index("tensor")
    y, x = dp // SIDE, dp % SIDE
    scale_out = 1.0 / math.sqrt(full_width)
    scale_value = 1.0 / math.sqrt(features)

    out_all = lax.all_gather(
        jnp.concatenate([w_out, basis_out.astype(BF)], axis=1), "tensor", axis=0, tiled=False
    )

    xf = tokens.astype(F32)
    normed = (xf * lax.rsqrt(jnp.mean(xf * xf, axis=1, keepdims=True) + epsilon)).astype(BF)
    split = normed.reshape(count, SIDE, SIDE, block)
    own_x = pick(split, x, 2).reshape(count, SIDE * block)
    own_y = pick(split, y, 1).reshape(count, SIDE * block)
    few = lax.dynamic_slice_in_dim(split, t * ROWS, ROWS, 0)
    piece = jnp.stack(
        [pick(few, (x + j) % SIDE, 2).reshape(ROWS, SIDE * block) for j in (1, 2, 3)]
        + [pick(few, (y + j) % SIDE, 1).reshape(ROWS, SIDE * block) for j in (1, 2, 3)]
    )
    few_x = lax.dynamic_slice_in_dim(tokens, t * ROWS, ROWS, 0).astype(F32)
    few_t = lax.dynamic_slice_in_dim(target, t * ROWS, ROWS, 0).astype(F32)
    diff = (few_x - few_t).reshape(ROWS, groups, block).transpose(1, 0, 2)
    rows, gqk, gvt, diffs = spread(
        piece,
        jnp.concatenate([w_query, w_key], axis=1),
        jnp.concatenate([w_value, basis_value.astype(BF)], axis=1),
        diff,
    )
    wide = SIDE * block
    rows_x = rows[:3].reshape(3 * count, wide)
    rows_y = rows[3:].reshape(3 * count, wide)
    gqk = gqk.reshape(wide, 2 * local_width)
    gvt = gvt.reshape(wide, 2 * local_width)

    def dot(a, b):
        return jnp.dot(a, b, preferred_element_type=F32)

    qk_else = dot(rows_x, gqk).astype(BF).reshape(3, count, 2 * local_width)
    vt_else = dot(rows_y, gvt).astype(BF).reshape(3, count, 2 * local_width)
    qk_got, vt_got = swap(4, -1, False, qk_else, vt_else)
    qk = dot(own_x, gqk) + jnp.sum(qk_got.astype(F32), axis=0)
    vt = dot(own_y, gvt) + jnp.sum(vt_got.astype(F32), axis=0)
    shape3 = (count, heads_here, HEAD_DIM)
    query = qk[:, :local_width].astype(BF).reshape(shape3)
    keys = qk[:, local_width:].astype(BF).reshape(shape3)
    values = vt[:, :local_width].astype(BF).reshape(shape3)
    tangent_values = (vt[:, local_width:] / math.sqrt(features)).astype(BF).reshape(shape3)

    scores = (
        jnp.einsum("thd,shd->ths", query, keys, preferred_element_type=F32) / math.sqrt(HEAD_DIM)
        + pair_bias
    )
    at_row = lax.broadcasted_iota(jnp.int32, (count, count), 0)
    at_col = lax.broadcasted_iota(jnp.int32, (count, count), 1)
    allowed = (neighbours == 1) | (jnp.abs(at_row - at_col) <= 1)
    scores = jnp.where(allowed[:, None, :], scores, -jnp.inf)
    probs = jax.nn.softmax(scores, axis=2).astype(BF)
    mixed = jnp.einsum("ths,shd->thd", probs, values, preferred_element_type=F32)
    tangent_mixed = jnp.einsum("ths,shd->thd", probs, tangent_values, preferred_element_type=F32)
    mix = jnp.concatenate(
        [
            mixed.astype(BF).reshape(count, local_width),
            tangent_mixed.astype(BF).reshape(count, local_width),
        ],
        axis=1,
    )

    full = spread_mix(mix).reshape(groups, 16, ROWS, 2 * local_width)
    full = full.transpose(0, 2, 1, 3).reshape(groups * ROWS, 16, 2, local_width)
    mixed_all = full[:, :, 0].reshape(groups * ROWS, full_width)
    tangent_all = full[:, :, 1].reshape(groups * ROWS, full_width)
    out_all = out_all.reshape(full_width, 2 * block)
    out_full, tangent_out = out_all[:, :block], out_all[:, block:]
    attn = dot(mixed_all, out_full)
    tangent_attn = dot(mixed_all, tangent_out) * scale_out + dot(tangent_all, out_full)
    factor = loss_gain * full_width / total_tokens
    error = ((diffs.reshape(groups * ROWS, block) + attn) * factor).astype(BF)
    tangent_error = (tangent_attn * factor).astype(BF)

    back_part = jnp.einsum(
        "td,ad->ta", tangent_error, out_full, preferred_element_type=F32
    ) + scale_out * jnp.einsum("td,ad->ta", error, tangent_out, preferred_element_type=F32)
    curv_out_part = (
        jnp.einsum("ta,td->ad", tangent_all, error, preferred_element_type=F32)
        + jnp.einsum("ta,td->ad", mixed_all, tangent_error, preferred_element_type=F32)
    ) * scale_out
    curv_out = lax.psum_scatter(
        curv_out_part.astype(BF), "tensor", scatter_dimension=0, tiled=True
    ).astype(F32)
    back_tangent = collect_back(
        back_part.astype(BF).reshape(SIDE, SIDE, ROWS, full_width)
    ).reshape(shape3)

    value_back = (
        jnp.einsum("ths,thd->shd", probs, back_tangent, preferred_element_type=F32)
        .astype(BF)
        .reshape(count, local_width)
    )
    back_x, back_y = value_back[:, :HEAD_DIM], value_back[:, HEAD_DIM:]
    got_x, got_y = swap(5, 1, True, back_x, back_y)

    def outer(own, rest, mine, got):
        return (
            jnp.einsum("td,ta->da", own, mine, preferred_element_type=F32)
            + jnp.einsum(
                "td,ta->da", rest, got.reshape(3 * count, HEAD_DIM), preferred_element_type=F32
            )
        ) * scale_value

    curv_x = outer(own_x, rows_x, back_x, got_x).reshape(SIDE, block, HEAD_DIM)
    curv_y = outer(own_y, rows_y, back_y, got_y).reshape(SIDE, block, HEAD_DIM)

    def others(array, mine):
        return jnp.stack([pick(array, (mine + j) % SIDE, 0) for j in (1, 2, 3)]).astype(BF)

    sum_y, sum_x = swap(6, 1, False, others(curv_y, x), others(curv_x, y))
    curv_value = jnp.concatenate(
        [
            pick(curv_x, y, 0) + jnp.sum(sum_x.astype(F32), axis=0),
            pick(curv_y, x, 0) + jnp.sum(sum_y.astype(F32), axis=0),
        ],
        axis=1,
    )
    entries = 2.0 * features * full_width
    return finish(
        entries, curv_value, curv_out, basis_value, basis_out, prior_value, prior_out, prior_beta
    )


def solution(mesh):
    placed = (
        P("dp", None),
        P("dp", None),
        P("dp", "tensor", None),
        P("dp", None),
        P("dp", "tensor"),
        P("dp", "tensor"),
        P("dp", "tensor"),
        P("tensor", "dp"),
        P("dp", "tensor"),
        P("tensor", "dp"),
        P("dp", "tensor"),
        P("tensor", "dp"),
        P(),
    )
    return jax.shard_map(
        body,
        mesh=mesh,
        in_specs=placed,
        out_specs=(P("dp", "tensor"), P("tensor", "dp"), P()),
        check_vma=False,
    )
```

time: 825 us -> 315 us (0.38)
  waiting for transfers between devices: 590 us -> 1.65 us
  Pallas kernels: 0 us -> 196 us
  blocking collectives: 150 us -> 0 us
  local copies, waits for them, and re-layouts: 5.35 us -> 68.2 us
  matrix products: 45.7 us -> 25.5 us
    all_gather x6 -> x1, waiting for transfers between devices: 310 us -> 0.02 us  [body(): lax.all_gather(jnp.concatenate([w_out, basis_out.astype(BF)], axis=1), 't...]
    pallas_call x0 -> x7, Pallas kernels: none -> 196 us  [call(): pl.pallas_call(kernel, out_shape=out_shape, in_specs=in_specs or [VMEM] *...]
    psum x2 -> x0, blocking collectives: 150 us -> none  [the longest x1 77.2 us: body(): lax.psum(jnp.sum(basis_value * curv_value) + jnp.sum(basis_out * curv_out...]
    reduce_scatter x2 -> x1, waiting for transfers between devices: 150 us -> 1.59 us  [body(): lax.psum_scatter(curv_out_part.astype(BF), 'tensor', scatter_dimension=0,...]
    psum x1 -> x0, waiting for transfers between devices: 128 us -> none  [body(): lax.psum(partial_value.astype(jnp.bfloat16), 'tensor').astype(jnp.float32)]
    slice x0 -> x6, local copies, waits for them, and re-layouts: none -> 37.2 us  [the longest x2 23.2 us: body(): tangent_all = full[:, :, 1].reshape(groups * ROWS, full_width)]
    dot_general x14 -> x17, matrix products: 42.6 us -> 25 us  [the longest x7 10.5 us: dot(): return jnp.dot(a, b, preferred_element_type=F32)]
    reshape x0 -> x8, local copies, waits for them, and re-layouts: none -> 12.3 us  [the longest x1 6.96 us: body(): full = full.transpose(0, 2, 1, 3).reshape(groups * ROWS, 16, 2, local_width)]
  transfers between devices with their start and end apart: 9 -> 2, of which waited for: 9 -> 1; matrix products, arithmetic and copies ran while one was open for 5% -> 25% of each run, Pallas kernels for 0% -> 53%
where the time goes in v1:
time: 315 us; the launch traced here: 314 us
  Pallas kernels  196 us (62%)
  local copies, waits for them, and re-layouts  68.2 us (22%)
  matrix products  25.5 us (8%)
  between operations  15.6 us (5%)
  other arithmetic  6.91 us (2%)
    pallas_call x7, Pallas kernels, call(): pl.pallas_call(kernel, out_shape=out_shape, in_specs=in_specs or [VMEM] *...  196 us
    slice x2, local copies, waits for them, and re-layouts, body(): tangent_all = full[:, :, 1].reshape(groups * ROWS, full_width)  23.2 us
    unnamed x55, local copies, waits for them, and re-layouts  12 us
    dot_general x7, matrix products, dot(): return jnp.dot(a, b, preferred_element_type=F32)  10.5 us
    slice x1, local copies, waits for them, and re-layouts, body(): mixed_all = full[:, :, 0].reshape(groups * ROWS, full_width)  10.4 us
    reshape x1, local copies, waits for them, and re-layouts, body(): full = full.transpose(0, 2, 1, 3).reshape(groups * ROWS, 16, 2, local_width)  6.96 us
  transfers between devices with their start and end apart: 2, of which 1 were waited for; matrix products, arithmetic and copies ran while one was open for 25% of the time, Pallas kernels for 53%

profile of v1, /device:TPU:1, one launch (start us, length us, event | category | flops | bytes accessed | tf_op | source)
XLA Modules:
  0.0 314.3 jit_solution(10870402092013332536)
XLA Ops:
  7.2 1.0 convert_element_type.95
  8.2 1.7 pad_maximum_fusion.2
  10.2 3.2 %copy.58 = bf16[256,6144]{0,1:T(8,128)(2,1)S(1)} copy(bf16[256,6144]{1,0:T(8,128)(2,1)} %param.13) | data formatting | bytes 6291456 | tf_op args[0]
  13.4 2.0 copy.69
  15.5 0.8 copy.66
  16.3 0.8 fusion.1
  17.1 0.6 fusion.2
  17.8 1.7 copy-done.8
  19.5 0.5 constant_dynamic-slice_fusion.3
  20.5 2.1 constant_dynamic-slice_fusion
  23.1 1.1 convert_subtract_fusion
  24.3 62.5 %shard_map.148 = (bf16[6,16,16,1536]{3,2,1,0:T(8,128)(2,1)}, bf16[4,384,512]{2,1,0:T(8,128)(2,1)S(1)}, bf16[4,384,512]{2,1,0:T(8,128)(2,1)S(1)}, f32[16,16,384]{2,1,0:T(8,128)S(1)}) custom-call(bf16[6,16,1536]{2,1,0:T(8,128)(2,1)S(1)} %constant_dynamic-update-slice_fusion.piece, bf16[384,512]{1,0:T(8,128)(2,1)S(1)} %get-tuple-element.51.wqk, ...), custom_call_target="tpu_custom_call" | custom-call | tf_op jit(solution)/shard_map/pallas_call | solution.py:81
  86.8 2.9 fusion.54
  89.8 1.4 convolution_convert_fusion.1
  91.2 0.8 copy-done.6
  92.0 1.4 convolution_convert_fusion
  93.3 17.7 %shard_map.149 = (bf16[3,256,512]{2,1,0:T(8,128)(2,1)S(1)}, bf16[3,256,512]{2,1,0:T(8,128)(2,1)S(1)}) custom-call(bf16[3,256,512]{2,1,0:T(8,128)(2,1)S(1)} %bitcast.110, bf16[3,256,512]{2,1,0:T(8,128)(2,1)S(1)} %bitcast.111), custom_call_target="tpu_custom_call" | custom-call | tf_op jit(solution)/shard_map/pallas_call | solution.py:81
  111.0 1.2 constant_dynamic-slice_fusion.6
  112.3 0.6 convolution_add_fusion.3
  113.3 1.2 constant_dynamic-slice_fusion.7
  114.6 0.6 fusion.21
  117.0 43.1 %shard_map.150 = bf16[4,4,16,16,512]{4,3,2,1,0:T(8,128)(2,1)S(1)} custom-call(bf16[256,512]{1,0:T(8,128)(2,1)S(1)} %pad_maximum_fusion.6.mix), custom_call_target="tpu_custom_call" | custom-call | tf_op jit(solution)/shard_map/pallas_call | solution.py:81
  160.1 4.9 %copy.117 = bf16[16,16,16,512]{3,1,2,0:T(8,128)(2,1)} copy(bf16[16,16,16,512]{3,2,1,0:T(8,128)(2,1)S(1)} %bitcast.103) | data formatting | bytes 8388608 | tf_op jit(solution)/shard_map/reshape | solution.py:572
  164.9 7.0 %reshape.126 = bf16[256,16,2,256]{3,2,1,0:T(2,128)(2,1)} reshape(bf16[16,16,16,512]{3,2,1,0:T(8,128)(2,1)} %bitcast.119) | data formatting | bytes 8388608 | tf_op jit(solution)/shard_map/reshape | solution.py:573
  171.9 14.3 %fusion.55 = (bf16[256,16,1,256]{3,2,1,0:T(2,128)(2,1)}, bf16[256,16,1,256]{3,2,1,0:T(2,128)(2,1)}) fusion(bf16[256,16,2,256]{3,2,1,0:T(2,128)(2,1)} %reshape.126), kind=kLoop, calls=%fused_computation.99 | loop fusion | bytes 8388608 | tf_op jit(solution)/shard_map/slice | solution.py:575
  186.2 10.4 %copy.77 = bf16[256,16,1,256]{0,3,1,2:T(8,128)(2,1)} copy(bf16[256,16,1,256]{3,2,1,0:T(2,128)(2,1)} %get-tuple-element.32) | data formatting | bytes 4194304 | tf_op jit(solution)/shard_map/slice | solution.py:574
  196.7 8.9 %copy.78 = bf16[256,16,1,256]{0,3,1,2:T(8,128)(2,1)S(1)} copy(bf16[256,16,1,256]{3,2,1,0:T(2,128)(2,1)} %get-tuple-element.31) | data formatting | bytes 4194304 | tf_op jit(solution)/shard_map/slice | solution.py:575
  205.6 4.0 %fusion.37 = bf16[256,384]{1,0:T(8,128)(2,1)S(1)} fusion(f32[256,384]{1,0:T(8,128)S(1)} %bitcast.114, bf16[256,4096]{0,1:T(8,128)(2,1)} %bitcast.126, bf16[4096,768]{1,0:T(8,128)(2,1)} %all-gather.3.cloned.1.call-done), kind=kOutput, calls=%fused_computation.41 | convolution fusion | flops 805601280 | bytes 5832704 | tf_op jit(solution)/shard_map/dot_general | solution.py:540
  209.6 1.3 fusion.62
  211.1 0.6 slice-done.1
  211.8 1.3 fusion.34
  213.1 1.3 fusion.40
  214.4 3.0 multiply_convert_fusion
  218.0 3.2 %fusion.12 = f32[256,4096]{1,0:T(8,128)S(1)} fusion(bf16[256,384]{1,0:T(8,128)(2,1)S(1)} %fusion.40, bf16[4096,768]{1,0:T(8,128)(2,1)} %all-gather.3.cloned.1.call-done), kind=kOutput, calls=%fused_computation.19 | convolution fusion | flops 805306368 | bytes 7536640 | tf_op jit(solution)/shard_map/td,ad->ta/dot_general | solution.py:584
  221.2 3.2 %fusion.4 = bf16[256,4096]{1,0:T(8,128)(2,1)S(1)} fusion(f32[256,4096]{1,0:T(8,128)S(1)} %fusion.12, bf16[256,384]{1,0:T(8,128)(2,1)S(1)} %fusion.37, bf16[4096,768]{1,0:T(8,128)(2,1)} %all-gather.3.cloned.1.call-done), kind=kOutput, calls=%fused_computation.8 | convolution fusion | flops 808452096 | bytes 9633792 | tf_op jit(solution)/shard_map/td,ad->ta/dot_general | solution.py:586
  224.4 30.4 %shard_map.151 = bf16[16,16,256]{2,1,0:T(8,128)(2,1)S(1)} custom-call(bf16[4,4,16,4096]{3,2,1,0:T(8,128)(2,1)S(1)} %bitcast.104), custom_call_target="tpu_custom_call" | custom-call | tf_op jit(solution)/shard_map/pallas_call | solution.py:81
  255.3 6.4 %shard_map.152 = (bf16[3,256,128]{2,1,0:T(8,128)(2,1)S(1)}, bf16[3,256,128]{2,1,0:T(8,128)(2,1)S(1)}) custom-call(bf16[256,128]{1,0:T(8,128)(2,1)S(1)} %copy.96.refs_0_, bf16[256,128]{1,0:T(8,128)(2,1)S(1)} %copy.97.refs_1_), custom_call_target="tpu_custom_call" | custom-call | tf_op jit(solution)/shard_map/pallas_call | solution.py:81
  261.7 1.5 fusion.50
  263.3 0.8 fusion.8
  264.7 0.4 copy-done.5
  265.2 0.8 fusion.9
  266.2 7.1 %shard_map.153 = (bf16[3,384,128]{2,1,0:T(8,128)(2,1)S(1)}, bf16[3,384,128]{2,1,0:T(8,128)(2,1)S(1)}) custom-call(bf16[3,384,128]{2,1,0:T(8,128)(2,1)S(1)} %pad_maximum_fusion.4.refs_0_, bf16[3,384,128]{2,1,0:T(8,128)(2,1)S(1)} %pad_maximum_fusion.5.refs_1_), custom_call_target="tpu_custom_call" | custom-call | tf_op jit(solution)/shard_map/pallas_call | solution.py:81
  273.5 1.6 reduce-scatter.2.cloned.1.call-done
  275.1 1.0 convert_element_type.104.refs_1_
  276.1 29.3 %shard_map.154 = (f32[384,256]{1,0:T(8,128)S(1)}, f32[256,384]{1,0:T(8,128)S(1)}, f32[8,128]{1,0:T(8,128)S(1)}) custom-call(f32[384,256]{1,0:T(8,128)S(1)} %pad_maximum_fusion.3.refs_0_, f32[256,384]{1,0:T(8,128)S(1)} %convert_element_type.104.refs_1_, f32[384,256]{1,0:T(8,128)S(1)} %copy-done, f32[256,384]{1,0:T(8,128)S(1)} %copy-done.1, ...), custom_call_target="tpu_custom_call" | custom-call | tf_op jit(solution)/shard_map/pallas_call | solution.py:81
  305.4 0.6 slice_reduce_fusion
  306.0 0.7 copy.127
  306.7 0.7 copy.128
  (90 shorter events, 5.2 us)
Async XLA Ops:
  7.2 198.4 %all-gather.3.cloned.1.call-start = ((), (), s32[]{:S(2)}) async-start(), calls=%async_computation.2 | async-start | bytes 6684672 | tf_op jit(solution)/shard_map/all_gather | solution.py:510
  10.0 265.1 %reduce-scatter.2.cloned.1.call-start = ((), (), s32[]{:S(2)}) async-start(), calls=%async_computation.1 | async-start | bytes 3342336 | tf_op jit(solution)/shard_map/reduce_scatter | solution.py:591
  10.2 5.3 %copy-start.14 = (s32[256,256]{1,0:T(8,128)S(1)}, s32[256,256]{1,0:T(8,128)}, u32[]{:S(2)}) copy-start(s32[256,256]{1,0:T(8,128)} %param.16) | copy-start | bytes 786436
  17.8 1.8 copy-start.8
  19.5 3.5 %copy-start = (f32[384,256]{1,0:T(8,128)S(1)}, f32[384,256]{1,0:T(8,128)}, u32[]{:S(2)}) copy-start(f32[384,256]{1,0:T(8,128)} %refs_2_.1) | copy-start | bytes 1179652
  20.3 3.9 %copy-start.15 = (bf16[384,256]{1,0:T(8,128)(2,1)S(1)}, bf16[384,256]{1,0:T(8,128)(2,1)}, u32[]{:S(2)}) copy-start(bf16[384,256]{1,0:T(8,128)(2,1)} %param.18) | copy-start | bytes 589828
  20.3 3.9 %copy-start.16 = (bf16[384,256]{1,0:T(8,128)(2,1)S(1)}, bf16[384,256]{1,0:T(8,128)(2,1)}, u32[]{:S(2)}) copy-start(bf16[384,256]{1,0:T(8,128)(2,1)} %param.17) | copy-start | bytes 589828
  20.3 3.9 %copy-start.17 = (bf16[384,256]{1,0:T(8,128)(2,1)S(1)}, bf16[384,256]{1,0:T(8,128)(2,1)}, u32[]{:S(2)}) copy-start(bf16[384,256]{1,0:T(8,128)(2,1)} %param.19) | copy-start | bytes 589828
  89.7 1.4 copy-start.4
  89.8 2.2 copy-start.6
  112.2 0.9 copy-start.12
  113.3 2.2 copy-start.18
  114.5 1.0 copy-start.10
  114.6 1.2 copy-start.13
  205.6 5.3 %slice-start = ((s8[6291456]{0:T(1024)(128)(4,1)}), s8[4194304]{0:T(1024)(128)(4,1)S(1)}, s32[]{:S(2)}) async-start(s8[6291456]{0:T(1024)(128)(4,1)} %bitcast.133), calls=%async_computation.3 | async-start | bytes 8388608
  209.5 1.6 copy-start.9
  209.6 2.2 slice-start.1
  224.4 38.8 %copy-start.7 = (bf16[3,16,16,1536]{3,2,1,0:T(8,128)(2,1)S(1)}, bf16[3,16,16,1536]{3,2,1,0:T(8,128)(2,1)}, u32[]{:S(2)}) copy-start(bf16[3,16,16,1536]{3,2,1,0:T(8,128)(2,1)} %copy-done.6) | copy-start | bytes 7077892
  263.2 1.1 copy-start.11
  263.3 1.9 copy-start.5
  266.0 10.0 %copy-start.1 = (f32[256,384]{1,0:T(8,128)S(1)}, f32[256,384]{1,0:T(8,128)}, u32[]{:S(2)}) copy-start(f32[256,384]{1,0:T(8,128)} %refs_3_.1) | copy-start | bytes 1179652
  266.0 10.0 %copy-start.2 = (f32[384,256]{1,0:T(8,128)S(1)}, f32[384,256]{1,0:T(8,128)}, u32[]{:S(2)}) copy-start(f32[384,256]{1,0:T(8,128)} %refs_4_.1) | copy-start | bytes 1179652
  266.0 10.0 %copy-start.3 = (f32[256,384]{1,0:T(8,128)S(1)}, f32[256,384]{1,0:T(8,128)}, u32[]{:S(2)}) copy-start(f32[256,384]{1,0:T(8,128)} %refs_5_.1) | copy-start | bytes 1179652
Sparse Core Ops, SparseCore 0:
  10.4 65.3 all-gather.2
  217.5 57.5 reduce-scatter.1

commit v2 on v0

v2 whole, which is shorter than its diff:
```python
import math

import jax
import jax.numpy as jnp
from jax import lax
from jax.experimental import pallas as pl
from jax.experimental.pallas import tpu as pltpu
from jax.sharding import PartitionSpec as P

HEAD_DIM = 128
SIDE = 4
ROWS = 16

loss_gain = 32.0
epsilon = 1e-06

MESH = pl.DeviceIdType.MESH
BF = jnp.bfloat16
F32 = jnp.float32
VMEM = pl.BlockSpec(memory_space=pltpu.VMEM)
ANY = pl.BlockSpec(memory_space=pl.ANY)
SMEM = pl.BlockSpec(memory_space=pltpu.SMEM)
DMA = pltpu.SemaphoreType.DMA


def coords():
    dp = lax.axis_index("dp")
    t = lax.axis_index("tensor")
    return dp // SIDE, dp % SIDE, t


def at(y, x, t):
    return (((y + 2 * SIDE) % SIDE) * SIDE + (x + 2 * SIDE) % SIDE, (t + 32) % 16)


def along_x(j):
    y, x, t = coords()
    return at(y, x + j, t)


def along_y(j):
    y, x, t = coords()
    return at(y + j, x, t)


def along_t(k):
    y, x, t = coords()
    return at(y, x, t + k)


def along_z(k):
    y, x, t = coords()
    return at(y, x, t + 2 * k)


def other_core():
    y, x, t = coords()
    return at(y, x, t + 1 - 2 * (t % 2))


def greet(peers):
    barrier = pltpu.get_barrier_semaphore()
    for peer in peers:
        pl.semaphore_signal(barrier, inc=1, device_id=peer, device_id_type=MESH)
    pl.semaphore_wait(barrier, len(peers))


def send(src, dst, ssem, rsem, peer):
    copy = pltpu.make_async_remote_copy(
        src_ref=src,
        dst_ref=dst,
        send_sem=ssem,
        recv_sem=rsem,
        device_id=peer,
        device_id_type=MESH,
    )
    copy.start()
    return copy


NEAR = (1, 3, 2)
WIDE = 256
HALF = 128
BLOCK = 384
COUNT = 256


def dot(a, b):
    return jnp.dot(a, b, preferred_element_type=F32)


def dot_t(a, b):
    return lax.dot_general(a, b, (((1,), (1,)), ((), ())), preferred_element_type=F32)


def arrival(ref, ssem, rsem):
    y, x, t = coords()
    return pltpu.make_async_remote_copy(
        src_ref=ref,
        dst_ref=ref,
        send_sem=ssem,
        recv_sem=rsem,
        device_id=at(y, x, t + 2),
        device_id_type=MESH,
    )


class Ring:
    def __init__(self, slot, half, zs, zr, cs, cr):
        self.slot, self.half = slot, half
        self.zs, self.zr, self.cs, self.cr = zs, zr, cs, cr
        self.sent = []

    def start(self):
        y, x, t = coords()
        own = self.slot(t)
        for way in range(2):
            self.sent.append(
                send(own, own, self.zs.at[way, 0], self.zr.at[way, 0], along_z(1 - 2 * way))
            )
        self.sent.append(send(own, own, self.cs.at[0], self.cr.at[0], other_core()))

    def step(self, step):
        y, x, t = coords()
        for way in range(2):
            sign = 1 - 2 * way
            slot = (t - 2 * sign * step + 32) % 16
            got = self.slot(slot)
            arrival(got, self.zs.at[way, step - 1], self.zr.at[way, step - 1]).wait_recv()
            part = got if step < 3 else self.half(slot, way)
            self.sent.append(
                send(part, part, self.zs.at[way, step], self.zr.at[way, step], along_z(sign))
            )
            k = 2 * step - 1 + way
            self.sent.append(send(got, got, self.cs.at[k], self.cr.at[k], other_core()))

    def finish(self):
        y, x, t = coords()
        far = (t + 8) % 16
        for way in range(2):
            part = self.half(far, way)
            arrival(part, self.zs.at[way, 3], self.zr.at[way, 3]).wait_recv()
        got = self.slot(far)
        self.sent.append(send(got, got, self.cs.at[7], self.cr.at[7], other_core()))

    def settle(self):
        y, x, t = coords()
        for copy in self.sent:
            copy.wait_send()
        for k in range(8):
            step, way = (k + 1) // 2, (k + 1) % 2
            shift = 8 if k == 7 else 2 * step * (1 - 2 * way)
            got = self.slot((t + 1 - 2 * (t % 2) - shift + 32) % 16)
            arrival(got, self.cs.at[k], self.cr.at[k]).wait_recv()


def step_kernel(
    tokens, target, bias, near, wq, wk, wv, wo, bv, bo, pv, po, pb,
    nv, no, coef,
    tok16, tgt16, tok, n16, diff, diffs, rows, gqk, gvt, nx, ny, uall,
    bvv, bov, pvv, pov, nearv, biasv,
    pq, pt, rq, rv, accq, accv, qk, vt, probs, mix, full,
    acc1, acc2, err, terr, errt, terrt, bp, ra, rb, sa, sb, qa, qb, done, bt,
    co, rc, sc, rz, vb, gx, gy, cxf, cyf, cxb, cyb, hx, hy, cv, cw, one, two,
    ls, ps, pr, ws, wr, ds, dr, zs, zr, cs, cr, us, ur, vs, vr, xs, xr, ts, tr,
    as_, ar, bs, br, s1, r1, s2, r2, s3, r3, s4, r4, s5, r5, s6, r6, s7, r7, o1, i1, o2, i2,
):
    y, x, t = coords()
    c = t % 2
    z = t // 2
    me = y * SIDE + x
    full_width = 16 * WIDE
    features = 16 * BLOCK
    scale_out = 1.0 / math.sqrt(full_width)
    scale_value = 1.0 / math.sqrt(features)
    factor = loss_gain * full_width / (16 * COUNT)
    entries = 2.0 * features * full_width

    plane = [(i, j) for i in range(SIDE) for j in range(SIDE) if i or j]
    barrier = pltpu.get_barrier_semaphore()
    for i, j in plane:
        pl.semaphore_signal(barrier, inc=1, device_id=at(y + i, x + j, t), device_id_type=MESH)
    for k in range(1, 16):
        pl.semaphore_signal(barrier, inc=1, device_id=along_t(k), device_id_type=MESH)

    some = pl.ds(pl.multiple_of(t * ROWS, ROWS), ROWS)
    left, right = pl.ds(0, WIDE), pl.ds(WIDE, WIDE)
    loads = [
        (tokens.at[some], tok16),
        (target.at[some], tgt16),
        (wq, gqk.at[y, :, left]),
        (wk, gqk.at[y, :, right]),
        (wv, gvt.at[x, :, left]),
        (bv, bvv),
        (tokens, tok),
        (wo, uall.at[t, :, pl.ds(0, BLOCK)]),
        (bo, bov),
        (near, nearv),
        (bias, biasv),
        (pv, pvv),
        (po, pov),
    ]
    loads = [pltpu.make_async_copy(a, b, ls.at[k]) for k, (a, b) in enumerate(loads)]
    for copy in loads:
        copy.start()

    loads[0].wait()
    loads[1].wait()
    xf = tok16[...].astype(F32)
    inv = lax.rsqrt(jnp.mean(xf * xf, axis=1, keepdims=True) + epsilon)
    for k in range(16):
        cut = slice(k * BLOCK, (k + 1) * BLOCK)
        part = tok16[:, cut].astype(F32)
        n16[k // SIDE, k % SIDE] = (part * inv).astype(BF)
        diff[k] = part - tgt16[:, cut].astype(F32)
    pl.semaphore_wait(barrier, 30)

    pieces, weights, others = [], [], []
    for j in NEAR:
        pieces.append(
            send(n16.at[:, (x + j) % SIDE], rows.at[j - 1, t], ps.at[j - 1], pr.at[j - 1], along_x(j))
        )
        pieces.append(
            send(n16.at[(y + j) % SIDE], rows.at[j + 2, t], ps.at[j + 2], pr.at[j + 2], along_y(j))
        )
    for k in (2, 3, 4, 5):
        loads[k].wait()
    gvt[x, :, WIDE:] = bvv[...].astype(BF)
    for j in NEAR:
        weights.append(send(gqk.at[y], gqk.at[y], ws.at[j - 1], wr.at[j - 1], along_y(j)))
        weights.append(send(gvt.at[x], gvt.at[x], ws.at[j + 2], wr.at[j + 2], along_x(j)))
    for k, (i, j) in enumerate(plane):
        yy, xx = (y + i) % SIDE, (x + j) % SIDE
        others.append(
            send(diff.at[yy * SIDE + xx], diffs.at[me], ds.at[k], dr.at[k], (yy * SIDE + xx, t))
        )
    diffs[me] = diff[me]

    ring = Ring(
        lambda n: rows.at[:, n], lambda n, way: rows.at[pl.ds(3 * way, 3), n], zs, zr, cs, cr
    )
    for copy in pieces:
        copy.wait_recv()
    ring.start()

    loads[6].wait()

    def normalise(r, _):
        at_r = pl.ds(pl.multiple_of(r * ROWS, ROWS), ROWS)
        xf = tok[at_r].astype(F32)
        inv = lax.rsqrt(jnp.mean(xf * xf, axis=1, keepdims=True) + epsilon)
        for b in range(SIDE):
            cut = pl.ds(pl.multiple_of((b * SIDE + x) * BLOCK, HALF), BLOCK)
            nx[b, at_r] = (tok[at_r, cut].astype(F32) * inv).astype(BF)
            cut = pl.ds(pl.multiple_of((y * SIDE + b) * BLOCK, HALF), BLOCK)
            ny[b, at_r] = (tok[at_r, cut].astype(F32) * inv).astype(BF)
        return 0

    lax.fori_loop(0, COUNT // ROWS, normalise, 0)
    ring.step(1)
    loads[7].wait()
    loads[8].wait()
    uall[t, :, BLOCK:] = bov[...].astype(BF)
    ring.step(2)
    ring.step(3)
    for copy in weights:
        copy.wait_recv()
    for lhs, w, acc in ((nx, gqk, accq), (ny, gvt, accv)):
        total = dot(lhs[0], w[0])
        for b in range(1, SIDE):
            total = total + dot(lhs[b], w[b])
        acc[...] = total
    uring = Ring(
        lambda n: uall.at[n], lambda n, way: uall.at[n, pl.ds(HALF * way, HALF)], us, ur, vs, vr
    )
    ring.finish()
    uring.start()
    ring.settle()

    partial = []
    for j in NEAR:
        for w, k, out, got, peer in (
            (gqk, j - 1, pq, rq, along_x(-j)),
            (gvt, j + 2, pt, rv, along_y(-j)),
        ):
            total = dot(rows[k, :, 0].reshape(COUNT, BLOCK), w[0])
            for b in range(1, SIDE):
                total = total + dot(rows[k, :, b].reshape(COUNT, BLOCK), w[b])
            out[j - 1] = total.astype(BF)
            partial.append(send(out.at[j - 1], got.at[j - 1], xs.at[k], xr.at[k], peer))
    for copy in partial:
        copy.wait_recv()

    def add_up(r, _):
        at_r = pl.ds(pl.multiple_of(r * 32, 32), 32)
        total = accq[at_r]
        for j in range(3):
            total = total + rq[j, at_r].astype(F32)
        qk[at_r] = total.astype(BF)
        total = accv[at_r]
        for j in range(3):
            total = total + rv[j, at_r].astype(F32)
        vt[at_r, :WIDE] = total[:, :WIDE].astype(BF)
        vt[at_r, WIDE:] = (total[:, WIDE:] / math.sqrt(features)).astype(BF)
        return 0

    lax.fori_loop(0, COUNT // 32, add_up, 0)
    uring.step(1)

    loads[9].wait()
    loads[10].wait()
    at_row = lax.broadcasted_iota(jnp.int32, (COUNT, COUNT), 0)
    at_col = lax.broadcasted_iota(jnp.int32, (COUNT, COUNT), 1)
    allowed = (nearv[...] == 1) | (jnp.abs(at_row - at_col) <= 1)
    for h in range(2):
        cut = slice(h * HALF, (h + 1) * HALF)
        cut2 = slice(WIDE + h * HALF, WIDE + (h + 1) * HALF)
        scores = dot_t(qk[:, cut], qk[:, cut2]) / math.sqrt(HEAD_DIM) + biasv[h]
        scores = jnp.where(allowed, scores, -jnp.inf)
        e = jnp.exp(scores - jnp.max(scores, axis=1, keepdims=True))
        p = (e / jnp.sum(e, axis=1, keepdims=True)).astype(BF)
        probs[h] = p
        mix[:, cut] = dot(p, vt[:, cut]).astype(BF)
        mix[:, cut2] = dot(p, vt[:, cut2]).astype(BF)

    moved = []
    for k in range(1, 16):
        to = pl.ds(pl.multiple_of(((t + k) % 16) * ROWS, ROWS), ROWS)
        moved.append(send(mix.at[to], full.at[y, x, t], ts.at[k], tr.at[k], along_t(k)))
    full[y, x, t] = mix[some]
    for copy in moved:
        copy.wait_recv()
    low, high = pl.ds(0, 8), pl.ds(8, 8)
    first, second = [], []
    a, b = full.at[y, x, low], full.at[y, x, high]
    for j in NEAR:
        first.append(send(a, a, as_.at[0, j - 1], ar.at[0, j - 1], along_x(j)))
        first.append(send(b, b, bs.at[0, j - 1], br.at[0, j - 1], along_y(j)))
    for j in NEAR:
        second.append(send(a, a, as_.at[1, j - 1], ar.at[1, j - 1], along_y(j)))
        second.append(send(b, b, bs.at[1, j - 1], br.at[1, j - 1], along_x(j)))
    uring.step(2)
    for k, i in enumerate(NEAR):
        first[2 * k].wait_recv()
        first[2 * k + 1].wait_recv()
        a = full.at[y, (x - i + SIDE) % SIDE, low]
        b = full.at[(y - i + SIDE) % SIDE, x, high]
        for j in NEAR:
            second.append(send(a, a, as_.at[1 + i, j - 1], ar.at[1 + i, j - 1], along_y(j)))
            second.append(send(b, b, bs.at[1 + i, j - 1], br.at[1 + i, j - 1], along_x(j)))
    uring.step(3)
    uring.finish()
    uring.settle()
    for copy in second:
        copy.wait_recv()

    acc1[...] = jnp.zeros_like(acc1)
    acc2[...] = jnp.zeros_like(acc2)

    def forward(n, _):
        both = full[:, :, n].reshape(COUNT, 2 * WIDE)
        acc1[...] += dot(both[:, :WIDE], uall[n])
        acc2[...] += dot(both[:, WIDE:], uall[n, :, :BLOCK])
        return 0

    lax.fori_loop(0, 16, forward, 0)
    for copy in others:
        copy.wait_recv()
    err[...] = ((diffs[...].reshape(COUNT, BLOCK) + acc1[:, :BLOCK]) * factor).astype(BF)
    terr[...] = ((acc1[:, BLOCK:] * scale_out + acc2[...]) * factor).astype(BF)

    def backward(n, _):
        part = dot_t(terr[...], uall[n, :, :BLOCK]) + scale_out * dot_t(err[...], uall[n, :, BLOCK:])
        bp[n] = part.astype(BF).reshape(SIDE, SIDE, ROWS, WIDE)
        return 0

    lax.fori_loop(0, 16, backward, 0)
    first_b = []
    for j in NEAR:
        first_b.append(
            send(bp.at[low, (y + j) % SIDE], ra.at[j - 1], s1.at[0, j - 1], r1.at[0, j - 1], along_y(j))
        )
        first_b.append(
            send(bp.at[high, :, (x + j) % SIDE], rb.at[j - 1], s1.at[1, j - 1], r1.at[1, j - 1], along_x(j))
        )

    errt[...] = err[...].astype(F32).T.astype(BF)
    terrt[...] = terr[...].astype(F32).T.astype(BF)

    def outer(n, _):
        both = full[:, :, n].reshape(COUNT, 2 * WIDE)
        part = dot(errt[...], both[:, WIDE:]) + dot(terrt[...], both[:, :WIDE])
        co[n // 2, n % 2] = (part * scale_out).astype(BF)
        return 0

    lax.fori_loop(0, 16, outer, 0)
    swapped = send(co.at[:, 1 - c], rc, s7.at[0], r7.at[0], other_core())

    for copy in first_b:
        copy.wait_recv()
    for i in range(SIDE):
        total = bp[0:8, y, i].astype(F32)
        for j in range(3):
            total = total + ra[j, :, i].astype(F32)
        sa[i] = total.astype(BF)
        total = bp[8:16, i, x].astype(F32)
        for j in range(3):
            total = total + rb[j, :, i].astype(F32)
        sb[i] = total.astype(BF)
    second_b = []
    for j in NEAR:
        second_b.append(
            send(sa.at[(x + j) % SIDE], qa.at[j - 1], s2.at[0, j - 1], r2.at[0, j - 1], along_x(j))
        )
        second_b.append(
            send(sb.at[(y + j) % SIDE], qb.at[j - 1], s2.at[1, j - 1], r2.at[1, j - 1], along_y(j))
        )
    for copy in second_b:
        copy.wait_recv()
    total = sa[x].astype(F32)
    for j in range(3):
        total = total + qa[j].astype(F32)
    done[0:8] = total.astype(BF)
    total = sb[y].astype(F32)
    for j in range(3):
        total = total + qb[j].astype(F32)
    done[8:16] = total.astype(BF)
    third = []
    for k in range(1, 16):
        third.append(send(done.at[(t + k) % 16], bt.at[t], s3.at[k], r3.at[k], along_t(k)))
    bt[t] = done[t]

    swapped.wait_recv()

    def pair(k, _):
        sc[k] = (co[k, c].astype(F32) + rc[k].astype(F32)).astype(BF)
        return 0

    lax.fori_loop(0, 8, pair, 0)
    shares = []
    for k in (1, 7, 2, 6, 3, 5, 4):
        shares.append(send(sc.at[(z + k) % 8], rz.at[k - 1], s4.at[k], r4.at[k], along_z(k)))

    for copy in third:
        copy.wait_recv()
    back = bt[...].reshape(COUNT, WIDE).astype(F32).T.astype(BF)
    fourth = []
    for h in range(2):
        vb[h] = dot(back[h * HALF : (h + 1) * HALF], probs[h]).astype(BF)
        got, along = ((gx, along_x), (gy, along_y))[h]
        for j in NEAR:
            fourth.append(
                send(vb.at[h], got.at[j - 1], s5.at[h, j - 1], r5.at[h, j - 1], along(j))
            )
    for copy in fourth:
        copy.wait_recv()
    for b in range(SIDE):
        for h, own, got, outf, outb in ((0, nx, gx, cxf, cxb), (1, ny, gy, cyf, cyb)):
            total = dot(vb[h], own[b])
            for j in range(3):
                total = total + dot(got[j], rows[3 * h + j, :, b].reshape(COUNT, BLOCK))
            total = total * scale_value
            outf[b] = total
            outb[b] = total.astype(BF)
    fifth = []
    for j in NEAR:
        fifth.append(
            send(cxb.at[(y + j) % SIDE], hx.at[j - 1], s6.at[0, j - 1], r6.at[0, j - 1], along_y(j))
        )
        fifth.append(
            send(cyb.at[(x + j) % SIDE], hy.at[j - 1], s6.at[1, j - 1], r6.at[1, j - 1], along_x(j))
        )
    for copy in shares:
        copy.wait_recv()
    total = sc[z].astype(F32)
    for j in range(7):
        total = total + rz[j].astype(F32)
    cw[...] = total.T
    loads[11].wait()
    loads[12].wait()
    for copy in fifth:
        copy.wait_recv()
    for h, (own, got, mine) in enumerate(((cxf, hx, y), (cyf, hy, x))):
        total = own[mine]
        for j in range(3):
            total = total + got[j].astype(F32)
        cv[:, h * HALF : (h + 1) * HALF] = total.T

    def everywhere(value, turn):
        one[turn, t] = jnp.full((8, 128), value, F32)
        copies = []
        for k in range(1, 16):
            part = one.at[turn, t]
            copies.append(send(part, part, o1.at[turn, k], i1.at[turn, k], along_t(k)))
        for copy in copies:
            copy.wait()
        two[turn, me] = jnp.sum(one[turn], axis=0)
        copies = []
        for k, (i, j) in enumerate(plane):
            part = two.at[turn, me]
            copies.append(
                send(part, part, o2.at[turn, k], i2.at[turn, k], at(y + i, x + j, t))
            )
        for copy in copies:
            copy.wait()
        return jnp.sum(two[turn], axis=0)[0:1, 0:1] / entries

    beta_before = pb[0, 0]
    alpha = everywhere(jnp.sum(bvv[...] * cv[...]) + jnp.sum(bov[...] * cw[...]), 0)
    nv[...] = cv[...] - alpha * bvv[...] - beta_before * pvv[...]
    no[...] = cw[...] - alpha * bov[...] - beta_before * pov[...]
    squares = everywhere(jnp.sum(nv[...] * nv[...]) + jnp.sum(no[...] * no[...]), 1)
    beta = jnp.sqrt(squares + epsilon)
    nv[...] = nv[...] / beta
    no[...] = no[...] / beta
    coef[0:1] = jnp.broadcast_to(alpha, (1, 128))
    coef[1:2] = jnp.broadcast_to(beta, (1, 128))
    for copy in (
        pieces + weights + others + partial + moved + first + second + first_b + second_b
        + third + [swapped] + shares + fourth + fifth
    ):
        copy.wait_send()


def body(
    tokens,
    target,
    pair_bias,
    neighbours,
    w_query,
    w_key,
    w_value,
    w_out,
    basis_value,
    basis_out,
    prior_value,
    prior_out,
    prior_beta,
):
    def vm(dtype, *dims):
        return pltpu.VMEM(dims, dtype)

    features = 16 * BLOCK
    scratch = [
        vm(BF, ROWS, features),
        vm(BF, ROWS, features),
        vm(BF, COUNT, features),
        vm(BF, SIDE, SIDE, ROWS, BLOCK),
        vm(F32, 16, ROWS, BLOCK),
        vm(F32, 16, ROWS, BLOCK),
        vm(BF, 6, 16, SIDE, ROWS, BLOCK),
        vm(BF, SIDE, BLOCK, 2 * WIDE),
        vm(BF, SIDE, BLOCK, 2 * WIDE),
        vm(BF, SIDE, COUNT, BLOCK),
        vm(BF, SIDE, COUNT, BLOCK),
        vm(BF, 16, WIDE, 2 * BLOCK),
        vm(F32, BLOCK, WIDE),
        vm(F32, WIDE, BLOCK),
        vm(F32, BLOCK, WIDE),
        vm(F32, WIDE, BLOCK),
        vm(jnp.int32, COUNT, COUNT),
        vm(F32, 2, COUNT, COUNT),
        vm(BF, 3, COUNT, 2 * WIDE),
        vm(BF, 3, COUNT, 2 * WIDE),
        vm(BF, 3, COUNT, 2 * WIDE),
        vm(BF, 3, COUNT, 2 * WIDE),
        vm(F32, COUNT, 2 * WIDE),
        vm(F32, COUNT, 2 * WIDE),
        vm(BF, COUNT, 2 * WIDE),
        vm(BF, COUNT, 2 * WIDE),
        vm(BF, 2, COUNT, COUNT),
        vm(BF, COUNT, 2 * WIDE),
        vm(BF, SIDE, SIDE, 16, ROWS, 2 * WIDE),
        vm(F32, COUNT, 2 * BLOCK),
        vm(F32, COUNT, BLOCK),
        vm(BF, COUNT, BLOCK),
        vm(BF, COUNT, BLOCK),
        vm(BF, BLOCK, COUNT),
        vm(BF, BLOCK, COUNT),
        vm(BF, 16, SIDE, SIDE, ROWS, WIDE),
        vm(BF, 3, 8, SIDE, ROWS, WIDE),
        vm(BF, 3, 8, SIDE, ROWS, WIDE),
        vm(BF, SIDE, 8, ROWS, WIDE),
        vm(BF, SIDE, 8, ROWS, WIDE),
        vm(BF, 3, 8, ROWS, WIDE),
        vm(BF, 3, 8, ROWS, WIDE),
        vm(BF, 16, ROWS, WIDE),
        vm(BF, 16, ROWS, WIDE),
        vm(BF, 8, 2, BLOCK, WIDE),
        vm(BF, 8, BLOCK, WIDE),
        vm(BF, 8, BLOCK, WIDE),
        vm(BF, 7, BLOCK, WIDE),
        vm(BF, 2, HALF, COUNT),
        vm(BF, 3, HALF, COUNT),
        vm(BF, 3, HALF, COUNT),
        vm(F32, SIDE, HALF, BLOCK),
        vm(F32, SIDE, HALF, BLOCK),
        vm(BF, SIDE, HALF, BLOCK),
        vm(BF, SIDE, HALF, BLOCK),
        vm(BF, 3, HALF, BLOCK),
        vm(BF, 3, HALF, BLOCK),
        vm(F32, BLOCK, WIDE),
        vm(F32, WIDE, BLOCK),
        vm(F32, 2, 16, 8, 128),
        vm(F32, 2, 16, 8, 128),
        DMA((13,)),
        DMA((6,)), DMA((6,)),
        DMA((6,)), DMA((6,)),
        DMA((15,)), DMA((15,)),
        DMA((2, 4)), DMA((2, 4)), DMA((8,)), DMA((8,)),
        DMA((2, 4)), DMA((2, 4)), DMA((8,)), DMA((8,)),
        DMA((6,)), DMA((6,)),
        DMA((16,)), DMA((16,)),
        DMA((5, 3)), DMA((5, 3)), DMA((5, 3)), DMA((5, 3)),
        DMA((2, 3)), DMA((2, 3)),
        DMA((2, 3)), DMA((2, 3)),
        DMA((16,)), DMA((16,)),
        DMA((8,)), DMA((8,)),
        DMA((2, 3)), DMA((2, 3)),
        DMA((2, 3)), DMA((2, 3)),
        DMA((1,)), DMA((1,)),
        DMA((2, 16)), DMA((2, 16)), DMA((2, 15)), DMA((2, 15)),
    ]
    next_value, next_out, coef = pl.pallas_call(
        step_kernel,
        out_shape=(
            jax.ShapeDtypeStruct((BLOCK, WIDE), F32),
            jax.ShapeDtypeStruct((WIDE, BLOCK), F32),
            jax.ShapeDtypeStruct((8, 128), F32),
        ),
        in_specs=[ANY] * 12 + [SMEM],
        out_specs=(VMEM, VMEM, VMEM),
        scratch_shapes=scratch,
        compiler_params=pltpu.CompilerParams(
            collective_id=0, has_side_effects=True, vmem_limit_bytes=58 * 2**20
        ),
    )(
        tokens,
        target,
        pair_bias.transpose(1, 0, 2),
        neighbours,
        w_query,
        w_key,
        w_value,
        w_out,
        basis_value,
        basis_out,
        prior_value,
        prior_out,
        prior_beta.reshape(1, 1),
    )
    return next_value, next_out, coef[:2, 0]


def solution(mesh):
    placed = (
        P("dp", None),
        P("dp", None),
        P("dp", "tensor", None),
        P("dp", None),
        P("dp", "tensor"),
        P("dp", "tensor"),
        P("dp", "tensor"),
        P("tensor", "dp"),
        P("dp", "tensor"),
        P("tensor", "dp"),
        P("dp", "tensor"),
        P("tensor", "dp"),
        P(),
    )
    return jax.shard_map(
        body,
        mesh=mesh,
        in_specs=placed,
        out_specs=(P("dp", "tensor"), P("tensor", "dp"), P()),
        check_vma=False,
    )
```

time: 825 us -> 213 us (0.26)
  waiting for transfers between devices: 590 us -> 0 us
  Pallas kernels: 0 us -> 205 us
  blocking collectives: 150 us -> 0 us
  matrix products: 45.7 us -> 0 us
  between operations: 18.6 us -> 1.29 us
  other arithmetic: 13.4 us -> 0 us
    all_gather x6 -> x0, waiting for transfers between devices: 310 us -> none  [the longest x1 55.4 us: body(): lax.all_gather(basis_out.astype(jnp.bfloat16), 'dp', axis=1, tiled=True)]
    pallas_call x0 -> x1, Pallas kernels: none -> 205 us  [body(): pl.pallas_call(step_kernel, out_shape=(jax.ShapeDtypeStruct((BLOCK, WIDE)...]
    reduce_scatter x2 -> x0, waiting for transfers between devices: 150 us -> none  [the longest x1 82 us: body(): lax.psum_scatter(((first + second) * scale_out).astype(jnp.bfloat16), 'dp...]
    psum x2 -> x0, blocking collectives: 150 us -> none  [the longest x1 77.2 us: body(): lax.psum(jnp.sum(basis_value * curv_value) + jnp.sum(basis_out * curv_out...]
    psum x1 -> x0, waiting for transfers between devices: 128 us -> none  [body(): lax.psum(partial_value.astype(jnp.bfloat16), 'tensor').astype(jnp.float32)]
    dot_general x15 -> x0, matrix products: 43.5 us -> none  [the longest x4 13.7 us: body(): jnp.dot(normed, piece, preferred_element_type=jnp.float32)]
  transfers between devices with their start and end apart: 9 -> 0, of which waited for: 9 -> 0; matrix products, arithmetic and copies ran while one was open for 5% -> 0% of each run, Pallas kernels for 0% -> 0%
where the time goes in v2:
time: 213 us
  Pallas kernels  205 us (96%)
  local copies, waits for them, and re-layouts  6.71 us (3%)
    pallas_call x1, Pallas kernels, body(): pl.pallas_call(step_kernel, out_shape=(jax.ShapeDtypeStruct((BLOCK, WIDE)...  205 us
    unnamed x3, local copies, waits for them, and re-layouts  5.4 us

profile of v2, /device:TPU:1, one launch (start us, length us, event | category | flops | bytes accessed | tf_op | source)
XLA Modules:
  0.0 212.8 jit_solution(5480846214127848862)
XLA Ops:
  1.3 1.9 copy.19
  3.1 204.8 %shard_map.148 = (f32[384,256]{1,0:T(8,128)}, f32[256,384]{1,0:T(8,128)}, f32[8,128]{1,0:T(8,128)}) custom-call(bf16[256,6144]{1,0:T(8,128)(2,1)} %tokens.1, bf16[256,6144]{1,0:T(8,128)(2,1)} %target.1, f32[2,256,256]{2,1,0:T(8,128)} %bitcast.5, s32[256,256]{1,0:T(8,128)} %near.1, bf16[384,256]{1,0:T(8,128)(2,1)} %wq.1, bf16[384,256]{1,0:T(8,128)(2,1)} %wk.1, ...), custom_call_target="tpu_custom_call" | custom-call | tf_op jit(solution)/shard_map/pallas_call | solution.py:624
  208.0 1.3 slice_reduce_fusion
  209.3 1.8 copy.23
  211.1 1.8 copy.24

commit v3 on v2

--- a/solution.py
+++ b/solution.py
@@ -143,15 +143,74 @@
         got = self.slot(far)
         self.sent.append(send(got, got, self.cs.at[7], self.cr.at[7], other_core()))
 
-    def settle(self):
+    def cores(self, some):
         y, x, t = coords()
-        for copy in self.sent:
-            copy.wait_send()
-        for k in range(8):
+        for k in some:
             step, way = (k + 1) // 2, (k + 1) % 2
             shift = 8 if k == 7 else 2 * step * (1 - 2 * way)
             got = self.slot((t + 1 - 2 * (t % 2) - shift + 32) % 16)
             arrival(got, self.cs.at[k], self.cr.at[k]).wait_recv()
+
+    def settle(self):
+        for copy in self.sent:
+            copy.wait_send()
+
+
+class Sweep:
+    OFFSETS = (0, -1, 1, 2)
+
+    def __init__(self, part, full, sp, rp, ss, rs):
+        y, x, t = coords()
+        self.sent = []
+        self.sp, self.rp, self.ss, self.rs = sp, rp, ss, rs
+        self.first, self.then = (along_x, along_y) if part == 0 else (along_y, along_x)
+        self.base = 8 * part
+
+        def block(p, s, half=None):
+            rng = pl.ds(self.base, 8) if half is None else pl.ds(self.base + 4 * half, 4)
+            dy, dx = (s, p) if part == 0 else (p, s)
+            return full.at[(y + dy + SIDE) % SIDE, (x + dx + SIDE) % SIDE, rng]
+
+        self.block = block
+
+    def push(self, ref, ssem, rsem, peer):
+        self.sent.append(send(ref, ref, ssem, rsem, peer))
+
+    def start(self):
+        own = self.block(0, 0)
+        for k in range(2):
+            self.push(own, self.sp.at[k], self.rp.at[k], self.first(1 - 2 * k))
+
+    def across(self, q):
+        own = self.block(self.OFFSETS[q], 0)
+        for k in range(2):
+            self.push(own, self.ss.at[q, k], self.rs.at[q, k], self.then(1 - 2 * k))
+
+    def relay(self):
+        for k in range(2):
+            off = 2 * k - 1
+            arrival(self.block(off, 0), self.sp.at[k], self.rp.at[k]).wait_recv()
+            half = self.block(off, 0, k)
+            self.push(half, self.sp.at[2 + k], self.rp.at[2 + k], self.first(1 - 2 * k))
+
+    def relay_across(self, q):
+        p = self.OFFSETS[q]
+        for k in range(2):
+            off = 2 * k - 1
+            arrival(self.block(p, off), self.ss.at[q, k], self.rs.at[q, k]).wait_recv()
+            half = self.block(p, off, k)
+            self.push(half, self.ss.at[q, 2 + k], self.rs.at[q, 2 + k], self.then(1 - 2 * k))
+
+    def far(self):
+        for k in range(2):
+            arrival(self.block(2, 0, k), self.sp.at[2 + k], self.rp.at[2 + k]).wait_recv()
+
+    def last(self):
+        for q in range(4):
+            for k in range(2):
+                arrival(
+                    self.block(self.OFFSETS[q], 2, k), self.ss.at[q, 2 + k], self.rs.at[q, 2 + k]
+                ).wait_recv()
 
 
 def step_kernel(
@@ -161,7 +220,7 @@
     bvv, bov, pvv, pov, nearv, biasv,
     pq, pt, rq, rv, accq, accv, qk, vt, probs, mix, full,
     acc1, acc2, err, terr, errt, terrt, bp, ra, rb, sa, sb, qa, qb, done, bt,
-    co, rc, sc, rz, vb, gx, gy, cxf, cyf, cxb, cyb, hx, hy, cv, cw, one, two,
+    co, rc, sc, rz, tx, vb, gx, gy, cxf, cyf, cxb, cyb, hx, hy, cv, cw, one, two,
     ls, ps, pr, ws, wr, ds, dr, zs, zr, cs, cr, us, ur, vs, vr, xs, xr, ts, tr,
     as_, ar, bs, br, s1, r1, s2, r2, s3, r3, s4, r4, s5, r5, s6, r6, s7, r7, o1, i1, o2, i2,
 ):
@@ -196,12 +255,15 @@
         (wo, uall.at[t, :, pl.ds(0, BLOCK)]),
         (bo, bov),
         (near, nearv),
-        (bias, biasv),
+        (bias.at[:, 0], biasv.at[0]),
+        (bias.at[:, 1], biasv.at[1]),
         (pv, pvv),
         (po, pov),
     ]
     loads = [pltpu.make_async_copy(a, b, ls.at[k]) for k, (a, b) in enumerate(loads)]
-    for copy in loads:
+    for copy in loads[:2]:
+        copy.start()
+    for copy in loads[2:]:
         copy.start()
 
     loads[0].wait()
@@ -262,7 +324,6 @@
     loads[8].wait()
     uall[t, :, BLOCK:] = bov[...].astype(BF)
     ring.step(2)
-    ring.step(3)
     for copy in weights:
         copy.wait_recv()
     for lhs, w, acc in ((nx, gqk, accq), (ny, gvt, accv)):
@@ -270,45 +331,62 @@
         for b in range(1, SIDE):
             total = total + dot(lhs[b], w[b])
         acc[...] = total
+    ring.step(3)
+
+    order = []
+    for off in (0, -1, 1, -2, 2, -3, 3, 4):
+        base = ((z + off + 8) % 8) * 2
+        order += [base + c, base + 1 - c]
+    partial = []
+
+    def products(part, lo, hi):
+        for w, k0, out, got, along in ((gqk, 0, pq, rq, along_x), (gvt, 3, pt, rv, along_y)):
+            total = None
+            for b in range(SIDE):
+                lhs = jnp.concatenate(
+                    [rows[k0 + j, n, b] for j in range(3) for n in order[lo:hi]], axis=0
+                )
+                more = dot(lhs, w[b])
+                total = more if total is None else total + more
+            size = (hi - lo) * ROWS
+            for j in range(3):
+                out[j, lo * ROWS : hi * ROWS] = total[j * size : (j + 1) * size].astype(BF)
+            cut = pl.ds(lo * ROWS, size)
+            for j in NEAR:
+                sem = (part, k0 + j - 1)
+                partial.append(
+                    send(out.at[j - 1, cut], got.at[j - 1, cut], xs.at[sem], xr.at[sem], along(-j))
+                )
+
+    ring.cores(range(5))
+    products(0, 0, 10)
     uring = Ring(
         lambda n: uall.at[n], lambda n, way: uall.at[n, pl.ds(HALF * way, HALF)], us, ur, vs, vr
     )
     ring.finish()
     uring.start()
-    ring.settle()
-
-    partial = []
-    for j in NEAR:
-        for w, k, out, got, peer in (
-            (gqk, j - 1, pq, rq, along_x(-j)),
-            (gvt, j + 2, pt, rv, along_y(-j)),
-        ):
-            total = dot(rows[k, :, 0].reshape(COUNT, BLOCK), w[0])
-            for b in range(1, SIDE):
-                total = total + dot(rows[k, :, b].reshape(COUNT, BLOCK), w[b])
-            out[j - 1] = total.astype(BF)
-            partial.append(send(out.at[j - 1], got.at[j - 1], xs.at[k], xr.at[k], peer))
+    ring.cores(range(5, 8))
+    products(1, 10, 16)
+    uring.step(1)
     for copy in partial:
         copy.wait_recv()
 
-    def add_up(r, _):
-        at_r = pl.ds(pl.multiple_of(r * 32, 32), 32)
-        total = accq[at_r]
+    for p, n in enumerate(order):
+        at_n = pl.ds(pl.multiple_of(n * ROWS, ROWS), ROWS)
+        at_p = slice(p * ROWS, (p + 1) * ROWS)
+        total = accq[at_n]
         for j in range(3):
-            total = total + rq[j, at_r].astype(F32)
-        qk[at_r] = total.astype(BF)
-        total = accv[at_r]
+            total = total + rq[j, at_p].astype(F32)
+        qk[at_n] = total.astype(BF)
+        total = accv[at_n]
         for j in range(3):
-            total = total + rv[j, at_r].astype(F32)
-        vt[at_r, :WIDE] = total[:, :WIDE].astype(BF)
-        vt[at_r, WIDE:] = (total[:, WIDE:] / math.sqrt(features)).astype(BF)
-        return 0
-
-    lax.fori_loop(0, COUNT // 32, add_up, 0)
-    uring.step(1)
+            total = total + rv[j, at_p].astype(F32)
+        vt[at_n, :WIDE] = total[:, :WIDE].astype(BF)
+        vt[at_n, WIDE:] = (total[:, WIDE:] / math.sqrt(features)).astype(BF)
 
     loads[9].wait()
     loads[10].wait()
+    loads[11].wait()
     at_row = lax.broadcasted_iota(jnp.int32, (COUNT, COUNT), 0)
     at_col = lax.broadcasted_iota(jnp.int32, (COUNT, COUNT), 1)
     allowed = (nearv[...] == 1) | (jnp.abs(at_row - at_col) <= 1)
@@ -328,42 +406,48 @@
         to = pl.ds(pl.multiple_of(((t + k) % 16) * ROWS, ROWS), ROWS)
         moved.append(send(mix.at[to], full.at[y, x, t], ts.at[k], tr.at[k], along_t(k)))
     full[y, x, t] = mix[some]
+    uring.step(2)
     for copy in moved:
         copy.wait_recv()
-    low, high = pl.ds(0, 8), pl.ds(8, 8)
-    first, second = [], []
-    a, b = full.at[y, x, low], full.at[y, x, high]
-    for j in NEAR:
-        first.append(send(a, a, as_.at[0, j - 1], ar.at[0, j - 1], along_x(j)))
-        first.append(send(b, b, bs.at[0, j - 1], br.at[0, j - 1], along_y(j)))
-    for j in NEAR:
-        second.append(send(a, a, as_.at[1, j - 1], ar.at[1, j - 1], along_y(j)))
-        second.append(send(b, b, bs.at[1, j - 1], br.at[1, j - 1], along_x(j)))
-    uring.step(2)
-    for k, i in enumerate(NEAR):
-        first[2 * k].wait_recv()
-        first[2 * k + 1].wait_recv()
-        a = full.at[y, (x - i + SIDE) % SIDE, low]
-        b = full.at[(y - i + SIDE) % SIDE, x, high]
-        for j in NEAR:
-            second.append(send(a, a, as_.at[1 + i, j - 1], ar.at[1 + i, j - 1], along_y(j)))
-            second.append(send(b, b, bs.at[1 + i, j - 1], br.at[1 + i, j - 1], along_x(j)))
+    sweeps = [
+        Sweep(0, full, as_.at[0], ar.at[0], bs.at[0], br.at[0]),
+        Sweep(1, full, as_.at[1], ar.at[1], bs.at[1], br.at[1]),
+    ]
+    for sweep in sweeps:
+        sweep.start()
+    for sweep in sweeps:
+        sweep.across(0)
+    for sweep in sweeps:
+        sweep.relay()
+    for sweep in sweeps:
+        sweep.across(1)
+        sweep.across(2)
     uring.step(3)
+    for sweep in sweeps:
+        sweep.relay_across(0)
+    for sweep in sweeps:
+        sweep.far()
+        sweep.across(3)
     uring.finish()
-    uring.settle()
-    for copy in second:
-        copy.wait_recv()
+    for q in (1, 2, 3):
+        for sweep in sweeps:
+            sweep.relay_across(q)
+    uring.cores(range(8))
+    for sweep in sweeps:
+        sweep.last()
 
     acc1[...] = jnp.zeros_like(acc1)
     acc2[...] = jnp.zeros_like(acc2)
 
-    def forward(n, _):
-        both = full[:, :, n].reshape(COUNT, 2 * WIDE)
-        acc1[...] += dot(both[:, :WIDE], uall[n])
-        acc2[...] += dot(both[:, WIDE:], uall[n, :, :BLOCK])
+    def forward(k, _):
+        at_k = pl.ds(k * 4, 4)
+        parts = [full[:, :, k * 4 + i].reshape(COUNT, 2 * WIDE) for i in range(4)]
+        w = uall[at_k].reshape(4 * WIDE, 2 * BLOCK)
+        acc1[...] += dot(jnp.concatenate([p[:, :WIDE] for p in parts], axis=1), w)
+        acc2[...] += dot(jnp.concatenate([p[:, WIDE:] for p in parts], axis=1), w[:, :BLOCK])
         return 0
 
-    lax.fori_loop(0, 16, forward, 0)
+    lax.fori_loop(0, 4, forward, 0)
     for copy in others:
         copy.wait_recv()
     err[...] = ((diffs[...].reshape(COUNT, BLOCK) + acc1[:, :BLOCK]) * factor).astype(BF)
@@ -374,15 +458,16 @@
         bp[n] = part.astype(BF).reshape(SIDE, SIDE, ROWS, WIDE)
         return 0
 
-    lax.fori_loop(0, 16, backward, 0)
+    low, high = pl.ds(0, 8), pl.ds(8, 8)
     first_b = []
+    lax.fori_loop(0, 8, backward, 0)
     for j in NEAR:
-        first_b.append(
-            send(bp.at[low, (y + j) % SIDE], ra.at[j - 1], s1.at[0, j - 1], r1.at[0, j - 1], along_y(j))
-        )
-        first_b.append(
-            send(bp.at[high, :, (x + j) % SIDE], rb.at[j - 1], s1.at[1, j - 1], r1.at[1, j - 1], along_x(j))
-        )
+        src = bp.at[low, (y + j) % SIDE]
+        first_b.append(send(src, ra.at[j - 1], s1.at[0, j - 1], r1.at[0, j - 1], along_y(j)))
+    lax.fori_loop(8, 16, backward, 0)
+    for j in NEAR:
+        src = bp.at[high, :, (x + j) % SIDE]
+        first_b.append(send(src, rb.at[j - 1], s1.at[1, j - 1], r1.at[1, j - 1], along_x(j)))
 
     errt[...] = err[...].astype(F32).T.astype(BF)
     terrt[...] = terr[...].astype(F32).T.astype(BF)
@@ -415,6 +500,39 @@
         second_b.append(
             send(sb.at[(y + j) % SIDE], qb.at[j - 1], s2.at[1, j - 1], r2.at[1, j - 1], along_y(j))
         )
+
+    swapped.wait_recv()
+
+    def pair(k, _):
+        sc[k] = (co[k, c].astype(F32) + rc[k].astype(F32)).astype(BF)
+        return 0
+
+    lax.fori_loop(0, 8, pair, 0)
+    shares = []
+
+    def pass_on(step):
+        for way in range(2):
+            sign = 1 - 2 * way
+            slot = (z + sign * (4 - step) + 8) % 8
+            if step == 0:
+                cut = pl.ds(way * (BLOCK // 2), BLOCK // 2)
+                src, dst = sc.at[slot, cut], rz.at[way, 0, cut]
+            else:
+                shares[2 * (step - 1) + way].wait_recv()
+                if step == 1:
+                    a, b = way * (BLOCK // 2), (way + 1) * (BLOCK // 2)
+                    tx[way, 0] = sc[slot]
+                    total = sc[slot, a:b].astype(F32) + rz[way, 0, a:b].astype(F32)
+                    tx[way, 0, a:b] = total.astype(BF)
+                else:
+                    total = sc[slot].astype(F32) + rz[way, step - 1].astype(F32)
+                    tx[way, step - 1] = total.astype(BF)
+                src, dst = tx.at[way, step - 1], rz.at[way, step]
+            shares.append(
+                send(src, dst, s4.at[way, step], r4.at[way, step], along_z(sign))
+            )
+
+    pass_on(0)
     for copy in second_b:
         copy.wait_recv()
     total = sa[x].astype(F32)
@@ -430,17 +548,7 @@
         third.append(send(done.at[(t + k) % 16], bt.at[t], s3.at[k], r3.at[k], along_t(k)))
     bt[t] = done[t]
 
-    swapped.wait_recv()
-
-    def pair(k, _):
-        sc[k] = (co[k, c].astype(F32) + rc[k].astype(F32)).astype(BF)
-        return 0
-
-    lax.fori_loop(0, 8, pair, 0)
-    shares = []
-    for k in (1, 7, 2, 6, 3, 5, 4):
-        shares.append(send(sc.at[(z + k) % 8], rz.at[k - 1], s4.at[k], r4.at[k], along_z(k)))
-
+    pass_on(1)
     for copy in third:
         copy.wait_recv()
     back = bt[...].reshape(COUNT, WIDE).astype(F32).T.astype(BF)
@@ -452,6 +560,7 @@
             fourth.append(
                 send(vb.at[h], got.at[j - 1], s5.at[h, j - 1], r5.at[h, j - 1], along(j))
             )
+    pass_on(2)
     for copy in fourth:
         copy.wait_recv()
     for b in range(SIDE):
@@ -470,14 +579,9 @@
         fifth.append(
             send(cyb.at[(x + j) % SIDE], hy.at[j - 1], s6.at[1, j - 1], r6.at[1, j - 1], along_x(j))
         )
-    for copy in shares:
-        copy.wait_recv()
-    total = sc[z].astype(F32)
-    for j in range(7):
-        total = total + rz[j].astype(F32)
-    cw[...] = total.T
-    loads[11].wait()
+    pass_on(3)
     loads[12].wait()
+    loads[13].wait()
     for copy in fifth:
         copy.wait_recv()
     for h, (own, got, mine) in enumerate(((cxf, hx, y), (cyf, hy, x))):
@@ -485,41 +589,60 @@
         for j in range(3):
             total = total + got[j].astype(F32)
         cv[:, h * HALF : (h + 1) * HALF] = total.T
-
-    def everywhere(value, turn):
-        one[turn, t] = jnp.full((8, 128), value, F32)
-        copies = []
-        for k in range(1, 16):
-            part = one.at[turn, t]
-            copies.append(send(part, part, o1.at[turn, k], i1.at[turn, k], along_t(k)))
-        for copy in copies:
-            copy.wait()
-        two[turn, me] = jnp.sum(one[turn], axis=0)
-        copies = []
-        for k, (i, j) in enumerate(plane):
-            part = two.at[turn, me]
-            copies.append(
-                send(part, part, o2.at[turn, k], i2.at[turn, k], at(y + i, x + j, t))
-            )
-        for copy in copies:
-            copy.wait()
-        return jnp.sum(two[turn], axis=0)[0:1, 0:1] / entries
-
+    for copy in shares[6:]:
+        copy.wait_recv()
+    total = sc[z].astype(F32)
+    for way in range(2):
+        total = total + rz[way, 3].astype(F32)
+    cw[...] = total.T
+
+    def inner(a1, b1, a2, b2):
+        total = jnp.zeros((8, 128), F32)
+        for a, b in ((a1, b1), (a2, b2)):
+            prod = a[...] * b[...]
+            prod = jnp.sum(prod.reshape(prod.shape[0] // 8, 8, prod.shape[1]), axis=0)
+            for k in range(prod.shape[1] // 128):
+                total = total + prod[:, k * 128 : (k + 1) * 128]
+        return jnp.sum(total, axis=0, keepdims=True)
+
+    pairs = ((cv, bvv, cw, bov), (cv, cv, cw, cw), (cv, pvv, cw, pov))
+    pairs += ((bvv, bvv, bov, bov), (bvv, pvv, bov, pov), (pvv, pvv, pov, pov))
+    for k, args in enumerate(pairs):
+        one[t, k : k + 1] = inner(*args)
+    one[t, 6:8] = jnp.zeros((2, 128), F32)
+    rounds = []
+    for k in range(1, 16):
+        rounds.append(send(one.at[t], one.at[t], o1.at[k], i1.at[k], along_t(k)))
+    for copy in rounds:
+        copy.wait_recv()
+    two[me] = jnp.sum(one[...], axis=0)
+    for k, (i, j) in enumerate(plane):
+        peer = at(y + i, x + j, t)
+        rounds.append(send(two.at[me], two.at[me], o2.at[k], i2.at[k], peer))
+    for copy in rounds[15:]:
+        copy.wait_recv()
+    sums = jnp.sum(jnp.sum(two[...], axis=0), axis=1, keepdims=True) / entries
     beta_before = pb[0, 0]
-    alpha = everywhere(jnp.sum(bvv[...] * cv[...]) + jnp.sum(bov[...] * cw[...]), 0)
-    nv[...] = cv[...] - alpha * bvv[...] - beta_before * pvv[...]
-    no[...] = cw[...] - alpha * bov[...] - beta_before * pov[...]
-    squares = everywhere(jnp.sum(nv[...] * nv[...]) + jnp.sum(no[...] * no[...]), 1)
-    beta = jnp.sqrt(squares + epsilon)
-    nv[...] = nv[...] / beta
-    no[...] = no[...] / beta
+    cb, cc, cp, bb, bq, pp = (sums[k : k + 1] for k in range(6))
+    alpha = cb
+    squares = cc + alpha * alpha * bb + beta_before * beta_before * pp
+    squares = squares - 2.0 * (alpha * cb + beta_before * (cp - alpha * bq))
+    beta = jnp.sqrt(jnp.maximum(squares, 0.0) + epsilon)
+    scale = 1.0 / beta
+    nv[...] = (cv[...] - alpha * bvv[...] - beta_before * pvv[...]) * scale
+    no[...] = (cw[...] - alpha * bov[...] - beta_before * pov[...]) * scale
     coef[0:1] = jnp.broadcast_to(alpha, (1, 128))
     coef[1:2] = jnp.broadcast_to(beta, (1, 128))
     for copy in (
-        pieces + weights + others + partial + moved + first + second + first_b + second_b
-        + third + [swapped] + shares + fourth + fifth
+        pieces + weights + others + partial + moved + first_b + second_b
+        + third + [swapped] + shares + fourth + fifth + rounds
     ):
         copy.wait_send()
+    ring.settle()
+    uring.settle()
+    for sweep in sweeps:
+        for copy in sweep.sent:
+            copy.wait_send()
 
 
 def body(
@@ -589,7 +712,8 @@
         vm(BF, 8, 2, BLOCK, WIDE),
         vm(BF, 8, BLOCK, WIDE),
         vm(BF, 8, BLOCK, WIDE),
-        vm(BF, 7, BLOCK, WIDE),
+        vm(BF, 2, 4, BLOCK, WIDE),
+        vm(BF, 2, 3, BLOCK, WIDE),
         vm(BF, 2, HALF, COUNT),
         vm(BF, 3, HALF, COUNT),
         vm(BF, 3, HALF, COUNT),
@@ -601,25 +725,25 @@
         vm(BF, 3, HALF, BLOCK),
         vm(F32, BLOCK, WIDE),
         vm(F32, WIDE, BLOCK),
-        vm(F32, 2, 16, 8, 128),
-        vm(F32, 2, 16, 8, 128),
-        DMA((13,)),
+        vm(F32, 16, 8, 128),
+        vm(F32, 16, 8, 128),
+        DMA((14,)),
         DMA((6,)), DMA((6,)),
         DMA((6,)), DMA((6,)),
         DMA((15,)), DMA((15,)),
         DMA((2, 4)), DMA((2, 4)), DMA((8,)), DMA((8,)),
         DMA((2, 4)), DMA((2, 4)), DMA((8,)), DMA((8,)),
-        DMA((6,)), DMA((6,)),
+        DMA((2, 6)), DMA((2, 6)),
         DMA((16,)), DMA((16,)),
-        DMA((5, 3)), DMA((5, 3)), DMA((5, 3)), DMA((5, 3)),
+        DMA((2, 4)), DMA((2, 4)), DMA((2, 4, 4)), DMA((2, 4, 4)),
         DMA((2, 3)), DMA((2, 3)),
         DMA((2, 3)), DMA((2, 3)),
         DMA((16,)), DMA((16,)),
-        DMA((8,)), DMA((8,)),
+        DMA((2, 4)), DMA((2, 4)),
         DMA((2, 3)), DMA((2, 3)),
         DMA((2, 3)), DMA((2, 3)),
         DMA((1,)), DMA((1,)),
-        DMA((2, 16)), DMA((2, 16)), DMA((2, 15)), DMA((2, 15)),
+        DMA((16,)), DMA((16,)), DMA((15,)), DMA((15,)),
     ]
     next_value, next_out, coef = pl.pallas_call(
         step_kernel,
@@ -637,7 +761,7 @@
     )(
         tokens,
         target,
-        pair_bias.transpose(1, 0, 2),
+        pair_bias,
         neighbours,
         w_query,
         w_key,

time: 213 us -> 166 us (0.78)
  Pallas kernels: 205 us -> 160 us
    pallas_call x1, Pallas kernels: 205 us -> 160 us  [body(): pl.pallas_call(step_kernel, out_shape=(jax.ShapeDtypeStruct((BLOCK, WIDE)...]
    unnamed x3 -> x2, local copies, waits for them, and re-layouts: 5.4 us -> 3.53 us
where the time goes in v3:
time: 166 us
  Pallas kernels  160 us (96%)
  local copies, waits for them, and re-layouts  4.83 us (3%)
    pallas_call x1, Pallas kernels, body(): pl.pallas_call(step_kernel, out_shape=(jax.ShapeDtypeStruct((BLOCK, WIDE)...  160 us
    unnamed x2, local copies, waits for them, and re-layouts  3.53 us

profile of v3, /device:TPU:1, one launch (start us, length us, event | category | flops | bytes accessed | tf_op | source)
XLA Modules:
  0.0 165.9 jit_solution(655246705749809984)
XLA Ops:
  1.3 159.8 %shard_map.148 = (f32[384,256]{1,0:T(8,128)}, f32[256,384]{1,0:T(8,128)}, f32[8,128]{1,0:T(8,128)}) custom-call(bf16[256,6144]{1,0:T(8,128)(2,1)} %tokens.1, bf16[256,6144]{1,0:T(8,128)(2,1)} %target.1, f32[256,2,256]{2,1,0:T(2,128)} %bias.1, s32[256,256]{1,0:T(8,128)} %near.1, bf16[384,256]{1,0:T(8,128)(2,1)} %wq.1, bf16[384,256]{1,0:T(8,128)(2,1)} %wk.1, ...), custom_call_target="tpu_custom_call" | custom-call | tf_op jit(solution)/shard_map/pallas_call | solution.py:748
  161.1 1.3 slice_reduce_fusion
  162.4 1.8 %copy.19 = f32[384,256]{1,0:T(8,128)} copy(f32[384,256]{1,0:T(8,128)} %get-tuple-element.12) | data formatting | bytes 786432
  164.2 1.8 %copy.20 = f32[256,384]{1,0:T(8,128)} copy(f32[256,384]{1,0:T(8,128)} %get-tuple-element.13) | data formatting | bytes 786432

commit v4 on v3

--- a/solution.py
+++ b/solution.py
@@ -106,42 +106,49 @@
 
 
 class Ring:
-    def __init__(self, slot, half, zs, zr, cs, cr):
-        self.slot, self.half = slot, half
+    def __init__(self, slot, part, zs, zr, cs, cr):
+        self.slot, self.part = slot, part
         self.zs, self.zr, self.cs, self.cr = zs, zr, cs, cr
         self.sent = []
 
     def start(self):
         y, x, t = coords()
-        own = self.slot(t)
+        for i in range(2):
+            own = self.part(t, i)
+            for way in range(2):
+                sem = (way, 0, i)
+                self.sent.append(
+                    send(own, own, self.zs.at[sem], self.zr.at[sem], along_z(1 - 2 * way))
+                )
+        self.core(t, 0)
+
+    def core(self, slot, k):
+        got = self.slot(slot)
+        self.sent.append(send(got, got, self.cs.at[k], self.cr.at[k], other_core()))
+
+    def step(self, step, onward):
+        y, x, t = coords()
+        slots = [(t - 2 * (1 - 2 * way) * step + 32) % 16 for way in range(2)]
+        for i in range(2):
+            for way in range(2):
+                part = self.part(slots[way], i)
+                sem = (way, step - 1, i)
+                arrival(part, self.zs.at[sem], self.zr.at[sem]).wait_recv()
+                if i in onward[way]:
+                    sem = (way, step, i)
+                    self.sent.append(
+                        send(part, part, self.zs.at[sem], self.zr.at[sem], along_z(1 - 2 * way))
+                    )
         for way in range(2):
-            self.sent.append(
-                send(own, own, self.zs.at[way, 0], self.zr.at[way, 0], along_z(1 - 2 * way))
-            )
-        self.sent.append(send(own, own, self.cs.at[0], self.cr.at[0], other_core()))
-
-    def step(self, step):
-        y, x, t = coords()
-        for way in range(2):
-            sign = 1 - 2 * way
-            slot = (t - 2 * sign * step + 32) % 16
-            got = self.slot(slot)
-            arrival(got, self.zs.at[way, step - 1], self.zr.at[way, step - 1]).wait_recv()
-            part = got if step < 3 else self.half(slot, way)
-            self.sent.append(
-                send(part, part, self.zs.at[way, step], self.zr.at[way, step], along_z(sign))
-            )
-            k = 2 * step - 1 + way
-            self.sent.append(send(got, got, self.cs.at[k], self.cr.at[k], other_core()))
+            self.core(slots[way], 2 * step - 1 + way)
 
     def finish(self):
         y, x, t = coords()
         far = (t + 8) % 16
         for way in range(2):
-            part = self.half(far, way)
-            arrival(part, self.zs.at[way, 3], self.zr.at[way, 3]).wait_recv()
-        got = self.slot(far)
-        self.sent.append(send(got, got, self.cs.at[7], self.cr.at[7], other_core()))
+            sem = (way, 3, way)
+            arrival(self.part(far, way), self.zs.at[sem], self.zr.at[sem]).wait_recv()
+        self.core(far, 7)
 
     def cores(self, some):
         y, x, t = coords()
@@ -154,6 +161,9 @@
     def settle(self):
         for copy in self.sent:
             copy.wait_send()
+
+
+ALL, NONE = ((0, 1), (0, 1)), ((), ())
 
 
 class Sweep:
@@ -243,9 +253,12 @@
         pl.semaphore_signal(barrier, inc=1, device_id=along_t(k), device_id_type=MESH)
 
     some = pl.ds(pl.multiple_of(t * ROWS, ROWS), ROWS)
+    far = (t + 8) % 16
+    some_far = pl.ds(pl.multiple_of(far * ROWS, ROWS), ROWS)
     left, right = pl.ds(0, WIDE), pl.ds(WIDE, WIDE)
     loads = [
-        (tokens.at[some], tok16),
+        (tokens.at[some], tok16.at[0]),
+        (tokens.at[some_far], tok16.at[1]),
         (target.at[some], tgt16),
         (wq, gqk.at[y, :, left]),
         (wk, gqk.at[y, :, right]),
@@ -261,36 +274,42 @@
         (po, pov),
     ]
     loads = [pltpu.make_async_copy(a, b, ls.at[k]) for k, (a, b) in enumerate(loads)]
-    for copy in loads[:2]:
+    for copy in loads:
         copy.start()
-    for copy in loads[2:]:
-        copy.start()
-
-    loads[0].wait()
-    loads[1].wait()
-    xf = tok16[...].astype(F32)
-    inv = lax.rsqrt(jnp.mean(xf * xf, axis=1, keepdims=True) + epsilon)
-    for k in range(16):
-        cut = slice(k * BLOCK, (k + 1) * BLOCK)
-        part = tok16[:, cut].astype(F32)
-        n16[k // SIDE, k % SIDE] = (part * inv).astype(BF)
-        diff[k] = part - tgt16[:, cut].astype(F32)
+
+    for copy in loads[:3]:
+        copy.wait()
+    for i in range(2):
+        xf = tok16[i].astype(F32)
+        inv = lax.rsqrt(jnp.mean(xf * xf, axis=1, keepdims=True) + epsilon)
+        for k in range(16):
+            part = tok16[i, :, k * BLOCK : (k + 1) * BLOCK].astype(F32)
+            n16[i, k // SIDE, k % SIDE] = (part * inv).astype(BF)
+            if i == 0:
+                diff[k] = part - tgt16[:, k * BLOCK : (k + 1) * BLOCK].astype(F32)
     pl.semaphore_wait(barrier, 30)
 
     pieces, weights, others = [], [], []
-    for j in NEAR:
-        pieces.append(
-            send(n16.at[:, (x + j) % SIDE], rows.at[j - 1, t], ps.at[j - 1], pr.at[j - 1], along_x(j))
-        )
-        pieces.append(
-            send(n16.at[(y + j) % SIDE], rows.at[j + 2, t], ps.at[j + 2], pr.at[j + 2], along_y(j))
-        )
-    for k in (2, 3, 4, 5):
+
+    def pass_rows(i, slot):
+        for j in NEAR:
+            src, sem = n16.at[i, :, (x + j) % SIDE], (i, j - 1)
+            pieces.append(
+                send(src, rows.at[j - 1, slot], ps.at[sem], pr.at[sem], along_x(j))
+            )
+            src, sem = n16.at[i, (y + j) % SIDE], (i, j + 2)
+            pieces.append(
+                send(src, rows.at[j + 2, slot], ps.at[sem], pr.at[sem], along_y(j))
+            )
+
+    pass_rows(0, t)
+    for k in (3, 4, 5, 6):
         loads[k].wait()
     gvt[x, :, WIDE:] = bvv[...].astype(BF)
     for j in NEAR:
         weights.append(send(gqk.at[y], gqk.at[y], ws.at[j - 1], wr.at[j - 1], along_y(j)))
         weights.append(send(gvt.at[x], gvt.at[x], ws.at[j + 2], wr.at[j + 2], along_x(j)))
+    pass_rows(1, far)
     for k, (i, j) in enumerate(plane):
         yy, xx = (y + i) % SIDE, (x + j) % SIDE
         others.append(
@@ -299,13 +318,13 @@
     diffs[me] = diff[me]
 
     ring = Ring(
-        lambda n: rows.at[:, n], lambda n, way: rows.at[pl.ds(3 * way, 3), n], zs, zr, cs, cr
+        lambda n: rows.at[:, n], lambda n, i: rows.at[pl.ds(3 * i, 3), n], zs, zr, cs, cr
     )
-    for copy in pieces:
+    for copy in pieces[:6]:
         copy.wait_recv()
     ring.start()
 
-    loads[6].wait()
+    loads[7].wait()
 
     def normalise(r, _):
         at_r = pl.ds(pl.multiple_of(r * ROWS, ROWS), ROWS)
@@ -319,11 +338,14 @@
         return 0
 
     lax.fori_loop(0, COUNT // ROWS, normalise, 0)
-    ring.step(1)
-    loads[7].wait()
+    ring.step(1, ALL)
     loads[8].wait()
+    loads[9].wait()
     uall[t, :, BLOCK:] = bov[...].astype(BF)
-    ring.step(2)
+    ring.step(2, ALL)
+    for copy in pieces[6:]:
+        copy.wait_recv()
+    ring.core(far, 7)
     for copy in weights:
         copy.wait_recv()
     for lhs, w, acc in ((nx, gqk, accq), (ny, gvt, accv)):
@@ -331,10 +353,9 @@
         for b in range(1, SIDE):
             total = total + dot(lhs[b], w[b])
         acc[...] = total
-    ring.step(3)
 
     order = []
-    for off in (0, -1, 1, -2, 2, -3, 3, 4):
+    for off in (0, -1, 1, -2, 2, 4, -3, 3):
         base = ((z + off + 8) % 8) * 2
         order += [base + c, base + 1 - c]
     partial = []
@@ -358,16 +379,15 @@
                     send(out.at[j - 1, cut], got.at[j - 1, cut], xs.at[sem], xr.at[sem], along(-j))
                 )
 
-    ring.cores(range(5))
-    products(0, 0, 10)
+    ring.cores((0, 1, 2, 3, 4, 7))
+    products(0, 0, 12)
+    ring.step(3, NONE)
     uring = Ring(
-        lambda n: uall.at[n], lambda n, way: uall.at[n, pl.ds(HALF * way, HALF)], us, ur, vs, vr
+        lambda n: uall.at[n], lambda n, i: uall.at[n, pl.ds(HALF * i, HALF)], us, ur, vs, vr
     )
-    ring.finish()
     uring.start()
-    ring.cores(range(5, 8))
-    products(1, 10, 16)
-    uring.step(1)
+    ring.cores((5, 6))
+    products(1, 12, 16)
     for copy in partial:
         copy.wait_recv()
 
@@ -384,9 +404,9 @@
         vt[at_n, :WIDE] = total[:, :WIDE].astype(BF)
         vt[at_n, WIDE:] = (total[:, WIDE:] / math.sqrt(features)).astype(BF)
 
-    loads[9].wait()
     loads[10].wait()
     loads[11].wait()
+    loads[12].wait()
     at_row = lax.broadcasted_iota(jnp.int32, (COUNT, COUNT), 0)
     at_col = lax.broadcasted_iota(jnp.int32, (COUNT, COUNT), 1)
     allowed = (nearv[...] == 1) | (jnp.abs(at_row - at_col) <= 1)
@@ -406,7 +426,7 @@
         to = pl.ds(pl.multiple_of(((t + k) % 16) * ROWS, ROWS), ROWS)
         moved.append(send(mix.at[to], full.at[y, x, t], ts.at[k], tr.at[k], along_t(k)))
     full[y, x, t] = mix[some]
-    uring.step(2)
+    uring.step(1, ALL)
     for copy in moved:
         copy.wait_recv()
     sweeps = [
@@ -417,21 +437,24 @@
         sweep.start()
     for sweep in sweeps:
         sweep.across(0)
+    uring.step(2, ALL)
     for sweep in sweeps:
         sweep.relay()
     for sweep in sweeps:
         sweep.across(1)
         sweep.across(2)
-    uring.step(3)
     for sweep in sweeps:
         sweep.relay_across(0)
+    uring.step(3, ((0,), (1,)))
     for sweep in sweeps:
         sweep.far()
         sweep.across(3)
-    uring.finish()
-    for q in (1, 2, 3):
+    for q in (1, 2):
         for sweep in sweeps:
             sweep.relay_across(q)
+    uring.finish()
+    for sweep in sweeps:
+        sweep.relay_across(3)
     uring.cores(range(8))
     for sweep in sweeps:
         sweep.last()
@@ -458,16 +481,16 @@
         bp[n] = part.astype(BF).reshape(SIDE, SIDE, ROWS, WIDE)
         return 0
 
-    low, high = pl.ds(0, 8), pl.ds(8, 8)
     first_b = []
-    lax.fori_loop(0, 8, backward, 0)
-    for j in NEAR:
-        src = bp.at[low, (y + j) % SIDE]
-        first_b.append(send(src, ra.at[j - 1], s1.at[0, j - 1], r1.at[0, j - 1], along_y(j)))
-    lax.fori_loop(8, 16, backward, 0)
-    for j in NEAR:
-        src = bp.at[high, :, (x + j) % SIDE]
-        first_b.append(send(src, rb.at[j - 1], s1.at[1, j - 1], r1.at[1, j - 1], along_x(j)))
+    for part in range(2):
+        lax.fori_loop(4 * part, 4 * part + 4, backward, 0)
+        lax.fori_loop(8 + 4 * part, 12 + 4 * part, backward, 0)
+        low, high, here = pl.ds(4 * part, 4), pl.ds(8 + 4 * part, 4), pl.ds(4 * part, 4)
+        for j in NEAR:
+            src, sem = bp.at[low, (y + j) % SIDE], (part, 0, j - 1)
+            first_b.append(send(src, ra.at[j - 1, here], s1.at[sem], r1.at[sem], along_y(j)))
+            src, sem = bp.at[high, :, (x + j) % SIDE], (part, 1, j - 1)
+            first_b.append(send(src, rb.at[j - 1, here], s1.at[sem], r1.at[sem], along_x(j)))
 
     errt[...] = err[...].astype(F32).T.astype(BF)
     terrt[...] = terr[...].astype(F32).T.astype(BF)
@@ -481,25 +504,26 @@
     lax.fori_loop(0, 16, outer, 0)
     swapped = send(co.at[:, 1 - c], rc, s7.at[0], r7.at[0], other_core())
 
-    for copy in first_b:
-        copy.wait_recv()
-    for i in range(SIDE):
-        total = bp[0:8, y, i].astype(F32)
-        for j in range(3):
-            total = total + ra[j, :, i].astype(F32)
-        sa[i] = total.astype(BF)
-        total = bp[8:16, i, x].astype(F32)
-        for j in range(3):
-            total = total + rb[j, :, i].astype(F32)
-        sb[i] = total.astype(BF)
     second_b = []
-    for j in NEAR:
-        second_b.append(
-            send(sa.at[(x + j) % SIDE], qa.at[j - 1], s2.at[0, j - 1], r2.at[0, j - 1], along_x(j))
-        )
-        second_b.append(
-            send(sb.at[(y + j) % SIDE], qb.at[j - 1], s2.at[1, j - 1], r2.at[1, j - 1], along_y(j))
-        )
+    for part in range(2):
+        for copy in first_b[6 * part : 6 * part + 6]:
+            copy.wait_recv()
+        a, b = 4 * part, 4 * part + 4
+        for i in range(SIDE):
+            total = bp[a:b, y, i].astype(F32)
+            for j in range(3):
+                total = total + ra[j, a:b, i].astype(F32)
+            sa[i, a:b] = total.astype(BF)
+            total = bp[8 + a : 8 + b, i, x].astype(F32)
+            for j in range(3):
+                total = total + rb[j, a:b, i].astype(F32)
+            sb[i, a:b] = total.astype(BF)
+        here = pl.ds(a, 4)
+        for j in NEAR:
+            src, sem = sa.at[(x + j) % SIDE, here], (part, 0, j - 1)
+            second_b.append(send(src, qa.at[j - 1, here], s2.at[sem], r2.at[sem], along_x(j)))
+            src, sem = sb.at[(y + j) % SIDE, here], (part, 1, j - 1)
+            second_b.append(send(src, qb.at[j - 1, here], s2.at[sem], r2.at[sem], along_y(j)))
 
     swapped.wait_recv()
 
@@ -563,29 +587,31 @@
     pass_on(2)
     for copy in fourth:
         copy.wait_recv()
-    for b in range(SIDE):
-        for h, own, got, outf, outb in ((0, nx, gx, cxf, cxb), (1, ny, gy, cyf, cyb)):
+    fifth = []
+    for k in (2, 1, 3, 0):
+        for h, own, got, mine, outf, outb, to, along in (
+            (0, nx, gx, y, cxf, cxb, hx, along_y),
+            (1, ny, gy, x, cyf, cyb, hy, along_x),
+        ):
+            b = (mine + k) % SIDE
             total = dot(vb[h], own[b])
             for j in range(3):
                 total = total + dot(got[j], rows[3 * h + j, :, b].reshape(COUNT, BLOCK))
             total = total * scale_value
-            outf[b] = total
-            outb[b] = total.astype(BF)
-    fifth = []
-    for j in NEAR:
-        fifth.append(
-            send(cxb.at[(y + j) % SIDE], hx.at[j - 1], s6.at[0, j - 1], r6.at[0, j - 1], along_y(j))
-        )
-        fifth.append(
-            send(cyb.at[(x + j) % SIDE], hy.at[j - 1], s6.at[1, j - 1], r6.at[1, j - 1], along_x(j))
-        )
+            if k == 0:
+                outf[...] = total
+            else:
+                outb[k - 1] = total.astype(BF)
+                fifth.append(
+                    send(outb.at[k - 1], to.at[k - 1], s6.at[h, k - 1], r6.at[h, k - 1], along(k))
+                )
     pass_on(3)
-    loads[12].wait()
     loads[13].wait()
+    loads[14].wait()
     for copy in fifth:
         copy.wait_recv()
-    for h, (own, got, mine) in enumerate(((cxf, hx, y), (cyf, hy, x))):
-        total = own[mine]
+    for h, (own, got) in enumerate(((cxf, hx), (cyf, hy))):
+        total = own[...]
         for j in range(3):
             total = total + got[j].astype(F32)
         cv[:, h * HALF : (h + 1) * HALF] = total.T
@@ -628,11 +654,11 @@
     squares = cc + alpha * alpha * bb + beta_before * beta_before * pp
     squares = squares - 2.0 * (alpha * cb + beta_before * (cp - alpha * bq))
     beta = jnp.sqrt(jnp.maximum(squares, 0.0) + epsilon)
-    scale = 1.0 / beta
-    nv[...] = (cv[...] - alpha * bvv[...] - beta_before * pvv[...]) * scale
-    no[...] = (cw[...] - alpha * bov[...] - beta_before * pov[...]) * scale
+    nv[...] = cv[...] - alpha * bvv[...] - beta_before * pvv[...]
+    no[...] = cw[...] - alpha * bov[...] - beta_before * pov[...]
     coef[0:1] = jnp.broadcast_to(alpha, (1, 128))
     coef[1:2] = jnp.broadcast_to(beta, (1, 128))
+    coef[2:3] = jnp.broadcast_to(1.0 / beta, (1, 128))
     for copy in (
         pieces + weights + others + partial + moved + first_b + second_b
         + third + [swapped] + shares + fourth + fifth + rounds
@@ -643,6 +669,14 @@
     for sweep in sweeps:
         for copy in sweep.sent:
             copy.wait_send()
+
+
+def scale_kernel(rest_value, rest_out, coef, nv, no, out):
+    scale = coef[2:3, 0:1]
+    nv[...] = rest_value[...] * scale
+    no[...] = rest_out[...] * scale
+    out[0] = coef[0, 0]
+    out[1] = coef[1, 0]
 
 
 def body(
@@ -665,10 +699,10 @@
 
     features = 16 * BLOCK
     scratch = [
-        vm(BF, ROWS, features),
+        vm(BF, 2, ROWS, features),
         vm(BF, ROWS, features),
         vm(BF, COUNT, features),
-        vm(BF, SIDE, SIDE, ROWS, BLOCK),
+        vm(BF, 2, SIDE, SIDE, ROWS, BLOCK),
         vm(F32, 16, ROWS, BLOCK),
         vm(F32, 16, ROWS, BLOCK),
         vm(BF, 6, 16, SIDE, ROWS, BLOCK),
@@ -717,27 +751,27 @@
         vm(BF, 2, HALF, COUNT),
         vm(BF, 3, HALF, COUNT),
         vm(BF, 3, HALF, COUNT),
-        vm(F32, SIDE, HALF, BLOCK),
-        vm(F32, SIDE, HALF, BLOCK),
-        vm(BF, SIDE, HALF, BLOCK),
-        vm(BF, SIDE, HALF, BLOCK),
+        vm(F32, HALF, BLOCK),
+        vm(F32, HALF, BLOCK),
+        vm(BF, 3, HALF, BLOCK),
+        vm(BF, 3, HALF, BLOCK),
         vm(BF, 3, HALF, BLOCK),
         vm(BF, 3, HALF, BLOCK),
         vm(F32, BLOCK, WIDE),
         vm(F32, WIDE, BLOCK),
         vm(F32, 16, 8, 128),
         vm(F32, 16, 8, 128),
-        DMA((14,)),
-        DMA((6,)), DMA((6,)),
+        DMA((15,)),
+        DMA((2, 6)), DMA((2, 6)),
         DMA((6,)), DMA((6,)),
         DMA((15,)), DMA((15,)),
-        DMA((2, 4)), DMA((2, 4)), DMA((8,)), DMA((8,)),
-        DMA((2, 4)), DMA((2, 4)), DMA((8,)), DMA((8,)),
+        DMA((2, 3, 2)), DMA((2, 3, 2)), DMA((8,)), DMA((8,)),
+        DMA((2, 4, 2)), DMA((2, 4, 2)), DMA((8,)), DMA((8,)),
         DMA((2, 6)), DMA((2, 6)),
         DMA((16,)), DMA((16,)),
         DMA((2, 4)), DMA((2, 4)), DMA((2, 4, 4)), DMA((2, 4, 4)),
-        DMA((2, 3)), DMA((2, 3)),
-        DMA((2, 3)), DMA((2, 3)),
+        DMA((2, 2, 3)), DMA((2, 2, 3)),
+        DMA((2, 2, 3)), DMA((2, 2, 3)),
         DMA((16,)), DMA((16,)),
         DMA((2, 4)), DMA((2, 4)),
         DMA((2, 3)), DMA((2, 3)),
@@ -745,7 +779,7 @@
         DMA((1,)), DMA((1,)),
         DMA((16,)), DMA((16,)), DMA((15,)), DMA((15,)),
     ]
-    next_value, next_out, coef = pl.pallas_call(
+    rest_value, rest_out, coef = pl.pallas_call(
         step_kernel,
         out_shape=(
             jax.ShapeDtypeStruct((BLOCK, WIDE), F32),
@@ -773,7 +807,16 @@
         prior_out,
         prior_beta.reshape(1, 1),
     )
-    return next_value, next_out, coef[:2, 0]
+    return pl.pallas_call(
+        scale_kernel,
+        out_shape=(
+            jax.ShapeDtypeStruct((BLOCK, WIDE), F32),
+            jax.ShapeDtypeStruct((WIDE, BLOCK), F32),
+            jax.ShapeDtypeStruct((2,), F32),
+        ),
+        in_specs=[VMEM] * 3,
+        out_specs=(VMEM, VMEM, SMEM),
+    )(rest_value, rest_out, coef)
 
 
 def solution(mesh):

time: 166 us -> 153 us (0.922)
  Pallas kernels: 160 us -> 152 us
  local copies, waits for them, and re-layouts: 4.83 us -> 0 us
    pallas_call x1, Pallas kernels: 160 us -> 150 us  [body(): pl.pallas_call(step_kernel, out_shape=(jax.ShapeDtypeStruct((BLOCK, WIDE)...]
    unnamed x2 -> x0, local copies, waits for them, and re-layouts: 3.53 us -> none
    pallas_call x0 -> x1, Pallas kernels: none -> 2.06 us  [body(): pl.pallas_call(scale_kernel, out_shape=(jax.ShapeDtypeStruct((BLOCK, WIDE...]
where the time goes in v4:
time: 153 us
  Pallas kernels  152 us (99%)
    pallas_call x1, Pallas kernels, body(): pl.pallas_call(step_kernel, out_shape=(jax.ShapeDtypeStruct((BLOCK, WIDE)...  150 us

profile of v4, /device:TPU:1, one launch (start us, length us, event | category | flops | bytes accessed | tf_op | source)
XLA Modules:
  0.0 153.3 jit_solution(1382020972199593409)
XLA Ops:
  1.3 149.9 %shard_map.148 = (f32[384,256]{1,0:T(8,128)}, f32[256,384]{1,0:T(8,128)}, f32[8,128]{1,0:T(8,128)}) custom-call(bf16[256,6144]{1,0:T(8,128)(2,1)} %tokens.1, bf16[256,6144]{1,0:T(8,128)(2,1)} %target.1, f32[256,2,256]{2,1,0:T(2,128)} %bias.1, s32[256,256]{1,0:T(8,128)} %near.1, bf16[384,256]{1,0:T(8,128)(2,1)} %wq.1, bf16[384,256]{1,0:T(8,128)(2,1)} %wk.1, ...), custom_call_target="tpu_custom_call" | custom-call | tf_op jit(solution)/shard_map/pallas_call | solution.py:782
  151.2 2.1 %shard_map.149 = (f32[384,256]{1,0:T(8,128)}, f32[256,384]{1,0:T(8,128)}, f32[2]{0:T(128)}) custom-call(f32[384,256]{1,0:T(8,128)} %get-tuple-element.6.rest_value, f32[256,384]{1,0:T(8,128)} %get-tuple-element.7.rest_out, f32[8,128]{1,0:T(8,128)} %get-tuple-element.8.coef), custom_call_target="tpu_custom_call" | custom-call | tf_op jit(solution)/shard_map/pallas_call | solution.py:810

commit v5 on v4

--- a/solution.py
+++ b/solution.py
@@ -306,15 +306,19 @@
     for k in (3, 4, 5, 6):
         loads[k].wait()
     gvt[x, :, WIDE:] = bvv[...].astype(BF)
-    for j in NEAR:
-        weights.append(send(gqk.at[y], gqk.at[y], ws.at[j - 1], wr.at[j - 1], along_y(j)))
-        weights.append(send(gvt.at[x], gvt.at[x], ws.at[j + 2], wr.at[j + 2], along_x(j)))
+    lines = (
+        (gqk, y, along_y, 0),
+        (gvt, x, along_x, 1),
+    )
+
+    def pass_weights(held, mine, along, k, way, off, rng, sem):
+        ref = held.at[(mine + off + SIDE) % SIDE, rng]
+        weights.append(send(ref, ref, ws.at[k, sem], wr.at[k, sem], along(1 - 2 * way)))
+
+    for way in range(2):
+        for line in lines:
+            pass_weights(*line, way, 0, pl.ds(0, BLOCK), way)
     pass_rows(1, far)
-    for k, (i, j) in enumerate(plane):
-        yy, xx = (y + i) % SIDE, (x + j) % SIDE
-        others.append(
-            send(diff.at[yy * SIDE + xx], diffs.at[me], ds.at[k], dr.at[k], (yy * SIDE + xx, t))
-        )
     diffs[me] = diff[me]
 
     ring = Ring(
@@ -338,6 +342,11 @@
         return 0
 
     lax.fori_loop(0, COUNT // ROWS, normalise, 0)
+    for way in range(2):
+        for k, line in enumerate(lines):
+            weights[2 * way + k].wait_recv()
+            half = pl.ds(way * (BLOCK // 2), BLOCK // 2)
+            pass_weights(*line, way, 2 * way - 1, half, 2 + way)
     ring.step(1, ALL)
     loads[8].wait()
     loads[9].wait()
@@ -346,13 +355,8 @@
     for copy in pieces[6:]:
         copy.wait_recv()
     ring.core(far, 7)
-    for copy in weights:
-        copy.wait_recv()
-    for lhs, w, acc in ((nx, gqk, accq), (ny, gvt, accv)):
-        total = dot(lhs[0], w[0])
-        for b in range(1, SIDE):
-            total = total + dot(lhs[b], w[b])
-        acc[...] = total
+    for copy in weights[4:]:
+        copy.wait_recv()
 
     order = []
     for off in (0, -1, 1, -2, 2, 4, -3, 3):
@@ -381,6 +385,11 @@
 
     ring.cores((0, 1, 2, 3, 4, 7))
     products(0, 0, 12)
+    for lhs, w, acc in ((nx, gqk, accq), (ny, gvt, accv)):
+        total = dot(lhs[0], w[0])
+        for b in range(1, SIDE):
+            total = total + dot(lhs[b], w[b])
+        acc[...] = total
     ring.step(3, NONE)
     uring = Ring(
         lambda n: uall.at[n], lambda n, i: uall.at[n, pl.ds(HALF * i, HALF)], us, ur, vs, vr
@@ -403,6 +412,12 @@
             total = total + rv[j, at_p].astype(F32)
         vt[at_n, :WIDE] = total[:, :WIDE].astype(BF)
         vt[at_n, WIDE:] = (total[:, WIDE:] / math.sqrt(features)).astype(BF)
+
+    for k, (i, j) in enumerate(plane):
+        yy, xx = (y + i) % SIDE, (x + j) % SIDE
+        others.append(
+            send(diff.at[yy * SIDE + xx], diffs.at[me], ds.at[k], dr.at[k], (yy * SIDE + xx, t))
+        )
 
     loads[10].wait()
     loads[11].wait()
@@ -585,6 +600,21 @@
                 send(vb.at[h], got.at[j - 1], s5.at[h, j - 1], r5.at[h, j - 1], along(j))
             )
     pass_on(2)
+    loads[13].wait()
+    loads[14].wait()
+    def inner(a1, b1, a2, b2):
+        total = jnp.zeros((8, 128), F32)
+        for a, b in ((a1, b1), (a2, b2)):
+            prod = a[...] * b[...]
+            prod = jnp.sum(prod.reshape(prod.shape[0] // 8, 8, prod.shape[1]), axis=0)
+            for k in range(prod.shape[1] // 128):
+                total = total + prod[:, k * 128 : (k + 1) * 128]
+        return jnp.sum(total, axis=0, keepdims=True)
+
+    pairs = ((bvv, bvv, bov, bov), (bvv, pvv, bov, pov), (pvv, pvv, pov, pov))
+    for k, args in enumerate(pairs):
+        one[t, 3 + k : 4 + k] = inner(*args)
+    one[t, 6:8] = jnp.zeros((2, 128), F32)
     for copy in fourth:
         copy.wait_recv()
     fifth = []
@@ -606,8 +636,6 @@
                     send(outb.at[k - 1], to.at[k - 1], s6.at[h, k - 1], r6.at[h, k - 1], along(k))
                 )
     pass_on(3)
-    loads[13].wait()
-    loads[14].wait()
     for copy in fifth:
         copy.wait_recv()
     for h, (own, got) in enumerate(((cxf, hx), (cyf, hy))):
@@ -622,20 +650,9 @@
         total = total + rz[way, 3].astype(F32)
     cw[...] = total.T
 
-    def inner(a1, b1, a2, b2):
-        total = jnp.zeros((8, 128), F32)
-        for a, b in ((a1, b1), (a2, b2)):
-            prod = a[...] * b[...]
-            prod = jnp.sum(prod.reshape(prod.shape[0] // 8, 8, prod.shape[1]), axis=0)
-            for k in range(prod.shape[1] // 128):
-                total = total + prod[:, k * 128 : (k + 1) * 128]
-        return jnp.sum(total, axis=0, keepdims=True)
-
     pairs = ((cv, bvv, cw, bov), (cv, cv, cw, cw), (cv, pvv, cw, pov))
-    pairs += ((bvv, bvv, bov, bov), (bvv, pvv, bov, pov), (pvv, pvv, pov, pov))
     for k, args in enumerate(pairs):
         one[t, k : k + 1] = inner(*args)
-    one[t, 6:8] = jnp.zeros((2, 128), F32)
     rounds = []
     for k in range(1, 16):
         rounds.append(send(one.at[t], one.at[t], o1.at[k], i1.at[k], along_t(k)))
@@ -763,7 +780,7 @@
         vm(F32, 16, 8, 128),
         DMA((15,)),
         DMA((2, 6)), DMA((2, 6)),
-        DMA((6,)), DMA((6,)),
+        DMA((2, 4)), DMA((2, 4)),
         DMA((15,)), DMA((15,)),
         DMA((2, 3, 2)), DMA((2, 3, 2)), DMA((8,)), DMA((8,)),
         DMA((2, 4, 2)), DMA((2, 4, 2)), DMA((8,)), DMA((8,)),

time: 153 us -> 151 us (0.987)
  Pallas kernels: 152 us -> 149 us
    pallas_call x1, Pallas kernels: 150 us -> 147 us  [body(): pl.pallas_call(step_kernel, out_shape=(jax.ShapeDtypeStruct((BLOCK, WIDE)...]
where the time goes in v5:
time: 151 us
  Pallas kernels  149 us (99%)
    pallas_call x1, Pallas kernels, body(): pl.pallas_call(step_kernel, out_shape=(jax.ShapeDtypeStruct((BLOCK, WIDE)...  147 us

profile of v5, /device:TPU:1, one launch (start us, length us, event | category | flops | bytes accessed | tf_op | source)
XLA Modules:
  0.0 150.6 jit_solution(11898790046706358064)
XLA Ops:
  1.3 147.3 %shard_map.148 = (f32[384,256]{1,0:T(8,128)}, f32[256,384]{1,0:T(8,128)}, f32[8,128]{1,0:T(8,128)}) custom-call(bf16[256,6144]{1,0:T(8,128)(2,1)} %tokens.1, bf16[256,6144]{1,0:T(8,128)(2,1)} %target.1, f32[256,2,256]{2,1,0:T(2,128)} %bias.1, s32[256,256]{1,0:T(8,128)} %near.1, bf16[384,256]{1,0:T(8,128)(2,1)} %wq.1, bf16[384,256]{1,0:T(8,128)(2,1)} %wk.1, ...), custom_call_target="tpu_custom_call" | custom-call | tf_op jit(solution)/shard_map/pallas_call | solution.py:799
  148.6 2.1 %shard_map.149 = (f32[384,256]{1,0:T(8,128)}, f32[256,384]{1,0:T(8,128)}, f32[2]{0:T(128)}) custom-call(f32[384,256]{1,0:T(8,128)} %get-tuple-element.6.rest_value, f32[256,384]{1,0:T(8,128)} %get-tuple-element.7.rest_out, f32[8,128]{1,0:T(8,128)} %get-tuple-element.8.coef), custom_call_target="tpu_custom_call" | custom-call | tf_op jit(solution)/shard_map/pallas_call | solution.py:827

commit v6 on v5

--- a/solution.py
+++ b/solution.py
@@ -359,7 +359,7 @@
         copy.wait_recv()
 
     order = []
-    for off in (0, -1, 1, -2, 2, 4, -3, 3):
+    for off in (0, -1, 1, 4, -2, 2, -3, 3):
         base = ((z + off + 8) % 8) * 2
         order += [base + c, base + 1 - c]
     partial = []
@@ -383,8 +383,10 @@
                     send(out.at[j - 1, cut], got.at[j - 1, cut], xs.at[sem], xr.at[sem], along(-j))
                 )
 
-    ring.cores((0, 1, 2, 3, 4, 7))
-    products(0, 0, 12)
+    ring.cores((0, 1, 2, 7))
+    products(0, 0, 8)
+    ring.cores((3, 4))
+    products(1, 8, 12)
     for lhs, w, acc in ((nx, gqk, accq), (ny, gvt, accv)):
         total = dot(lhs[0], w[0])
         for b in range(1, SIDE):
@@ -396,7 +398,7 @@
     )
     uring.start()
     ring.cores((5, 6))
-    products(1, 12, 16)
+    products(2, 12, 16)
     for copy in partial:
         copy.wait_recv()
 
@@ -497,14 +499,16 @@
         return 0
 
     first_b = []
-    for part in range(2):
-        lax.fori_loop(4 * part, 4 * part + 4, backward, 0)
-        lax.fori_loop(8 + 4 * part, 12 + 4 * part, backward, 0)
-        low, high, here = pl.ds(4 * part, 4), pl.ds(8 + 4 * part, 4), pl.ds(4 * part, 4)
+    cuts = ((0, 3), (3, 8))
+    for part, (a, b) in enumerate(cuts):
+        here = pl.ds(a, b - a)
+        lax.fori_loop(a, b, backward, 0)
         for j in NEAR:
-            src, sem = bp.at[low, (y + j) % SIDE], (part, 0, j - 1)
+            src, sem = bp.at[here, (y + j) % SIDE], (part, 0, j - 1)
             first_b.append(send(src, ra.at[j - 1, here], s1.at[sem], r1.at[sem], along_y(j)))
-            src, sem = bp.at[high, :, (x + j) % SIDE], (part, 1, j - 1)
+        lax.fori_loop(8 + a, 8 + b, backward, 0)
+        for j in NEAR:
+            src, sem = bp.at[pl.ds(8 + a, b - a), :, (x + j) % SIDE], (part, 1, j - 1)
             first_b.append(send(src, rb.at[j - 1, here], s1.at[sem], r1.at[sem], along_x(j)))
 
     errt[...] = err[...].astype(F32).T.astype(BF)
@@ -520,10 +524,9 @@
     swapped = send(co.at[:, 1 - c], rc, s7.at[0], r7.at[0], other_core())
 
     second_b = []
-    for part in range(2):
+    for part, (a, b) in enumerate(cuts):
         for copy in first_b[6 * part : 6 * part + 6]:
             copy.wait_recv()
-        a, b = 4 * part, 4 * part + 4
         for i in range(SIDE):
             total = bp[a:b, y, i].astype(F32)
             for j in range(3):
@@ -533,7 +536,7 @@
             for j in range(3):
                 total = total + rb[j, a:b, i].astype(F32)
             sb[i, a:b] = total.astype(BF)
-        here = pl.ds(a, 4)
+        here = pl.ds(a, b - a)
         for j in NEAR:
             src, sem = sa.at[(x + j) % SIDE, here], (part, 0, j - 1)
             second_b.append(send(src, qa.at[j - 1, here], s2.at[sem], r2.at[sem], along_x(j)))
@@ -784,7 +787,7 @@
         DMA((15,)), DMA((15,)),
         DMA((2, 3, 2)), DMA((2, 3, 2)), DMA((8,)), DMA((8,)),
         DMA((2, 4, 2)), DMA((2, 4, 2)), DMA((8,)), DMA((8,)),
-        DMA((2, 6)), DMA((2, 6)),
+        DMA((3, 6)), DMA((3, 6)),
         DMA((16,)), DMA((16,)),
         DMA((2, 4)), DMA((2, 4)), DMA((2, 4, 4)), DMA((2, 4, 4)),
         DMA((2, 2, 3)), DMA((2, 2, 3)),

time: 151 us -> 150 us (level)
  no operation moved by 1% of the time
where the time goes in v6:
time: 150 us; the launch traced here: 149 us
  Pallas kernels  148 us (99%)
    pallas_call x1, Pallas kernels, body(): pl.pallas_call(step_kernel, out_shape=(jax.ShapeDtypeStruct((BLOCK, WIDE)...  146 us

profile of v6, /device:TPU:1, one launch (start us, length us, event | category | flops | bytes accessed | tf_op | source)
XLA Modules:
  0.0 149.4 jit_solution(1837859003226061197)
XLA Ops:
  1.3 146.1 %shard_map.148 = (f32[384,256]{1,0:T(8,128)}, f32[256,384]{1,0:T(8,128)}, f32[8,128]{1,0:T(8,128)}) custom-call(bf16[256,6144]{1,0:T(8,128)(2,1)} %tokens.1, bf16[256,6144]{1,0:T(8,128)(2,1)} %target.1, f32[256,2,256]{2,1,0:T(2,128)} %bias.1, s32[256,256]{1,0:T(8,128)} %near.1, bf16[384,256]{1,0:T(8,128)(2,1)} %wq.1, bf16[384,256]{1,0:T(8,128)(2,1)} %wk.1, ...), custom_call_target="tpu_custom_call" | custom-call | tf_op jit(solution)/shard_map/pallas_call | solution.py:802
  147.4 2.1 %shard_map.149 = (f32[384,256]{1,0:T(8,128)}, f32[256,384]{1,0:T(8,128)}, f32[2]{0:T(128)}) custom-call(f32[384,256]{1,0:T(8,128)} %get-tuple-element.6.rest_value, f32[256,384]{1,0:T(8,128)} %get-tuple-element.7.rest_out, f32[8,128]{1,0:T(8,128)} %get-tuple-element.8.coef), custom_call_target="tpu_custom_call" | custom-call | tf_op jit(solution)/shard_map/pallas_call | solution.py:830

commit v7 on v6

--- a/solution.py
+++ b/solution.py
@@ -78,7 +78,8 @@
     return copy
 
 
-NEAR = (1, 3, 2)
+NEAR = (2, 1, 3)
+AROUND = (8, 7, 9, 6, 10, 5, 11, 4, 12, 3, 13, 2, 14, 1, 15)
 WIDE = 256
 HALF = 128
 BLOCK = 384
@@ -245,11 +246,11 @@
     factor = loss_gain * full_width / (16 * COUNT)
     entries = 2.0 * features * full_width
 
-    plane = [(i, j) for i in range(SIDE) for j in range(SIDE) if i or j]
+    plane = [(i, j) for i in (2, 1, 3, 0) for j in (2, 1, 3, 0) if i or j]
     barrier = pltpu.get_barrier_semaphore()
     for i, j in plane:
         pl.semaphore_signal(barrier, inc=1, device_id=at(y + i, x + j, t), device_id_type=MESH)
-    for k in range(1, 16):
+    for k in AROUND:
         pl.semaphore_signal(barrier, inc=1, device_id=along_t(k), device_id_type=MESH)
 
     some = pl.ds(pl.multiple_of(t * ROWS, ROWS), ROWS)
@@ -439,7 +440,7 @@
         mix[:, cut2] = dot(p, vt[:, cut2]).astype(BF)
 
     moved = []
-    for k in range(1, 16):
+    for k in AROUND:
         to = pl.ds(pl.multiple_of(((t + k) % 16) * ROWS, ROWS), ROWS)
         moved.append(send(mix.at[to], full.at[y, x, t], ts.at[k], tr.at[k], along_t(k)))
     full[y, x, t] = mix[some]
@@ -454,12 +455,12 @@
         sweep.start()
     for sweep in sweeps:
         sweep.across(0)
-    uring.step(2, ALL)
     for sweep in sweeps:
         sweep.relay()
     for sweep in sweeps:
         sweep.across(1)
         sweep.across(2)
+    uring.step(2, ALL)
     for sweep in sweeps:
         sweep.relay_across(0)
     uring.step(3, ((0,), (1,)))
@@ -586,7 +587,7 @@
         total = total + qb[j].astype(F32)
     done[8:16] = total.astype(BF)
     third = []
-    for k in range(1, 16):
+    for k in AROUND:
         third.append(send(done.at[(t + k) % 16], bt.at[t], s3.at[k], r3.at[k], along_t(k)))
     bt[t] = done[t]
 
@@ -657,7 +658,7 @@
     for k, args in enumerate(pairs):
         one[t, k : k + 1] = inner(*args)
     rounds = []
-    for k in range(1, 16):
+    for k in AROUND:
         rounds.append(send(one.at[t], one.at[t], o1.at[k], i1.at[k], along_t(k)))
     for copy in rounds:
         copy.wait_recv()

time: 150 us -> 147 us (0.980)
  Pallas kernels: 148 us -> 146 us
    pallas_call x1, Pallas kernels: 146 us -> 144 us  [body(): pl.pallas_call(step_kernel, out_shape=(jax.ShapeDtypeStruct((BLOCK, WIDE)...]
where the time goes in v7:
time: 147 us
  Pallas kernels  146 us (99%)
    pallas_call x1, Pallas kernels, body(): pl.pallas_call(step_kernel, out_shape=(jax.ShapeDtypeStruct((BLOCK, WIDE)...  144 us

profile of v7, /device:TPU:1, one launch (start us, length us, event | category | flops | bytes accessed | tf_op | source)
XLA Modules:
  0.0 146.9 jit_solution(1693253047123581947)
XLA Ops:
  1.3 143.6 %shard_map.148 = (f32[384,256]{1,0:T(8,128)}, f32[256,384]{1,0:T(8,128)}, f32[8,128]{1,0:T(8,128)}) custom-call(bf16[256,6144]{1,0:T(8,128)(2,1)} %tokens.1, bf16[256,6144]{1,0:T(8,128)(2,1)} %target.1, f32[256,2,256]{2,1,0:T(2,128)} %bias.1, s32[256,256]{1,0:T(8,128)} %near.1, bf16[384,256]{1,0:T(8,128)(2,1)} %wq.1, bf16[384,256]{1,0:T(8,128)(2,1)} %wk.1, ...), custom_call_target="tpu_custom_call" | custom-call | tf_op jit(solution)/shard_map/pallas_call | solution.py:803
  144.9 2.1 %shard_map.149 = (f32[384,256]{1,0:T(8,128)}, f32[256,384]{1,0:T(8,128)}, f32[2]{0:T(128)}) custom-call(f32[384,256]{1,0:T(8,128)} %get-tuple-element.6.rest_value, f32[256,384]{1,0:T(8,128)} %get-tuple-element.7.rest_out, f32[8,128]{1,0:T(8,128)} %get-tuple-element.8.coef), custom_call_target="tpu_custom_call" | custom-call | tf_op jit(solution)/shard_map/pallas_call | solution.py:831

commit v8 on v7

--- a/solution.py
+++ b/solution.py
@@ -416,12 +416,6 @@
         vt[at_n, :WIDE] = total[:, :WIDE].astype(BF)
         vt[at_n, WIDE:] = (total[:, WIDE:] / math.sqrt(features)).astype(BF)
 
-    for k, (i, j) in enumerate(plane):
-        yy, xx = (y + i) % SIDE, (x + j) % SIDE
-        others.append(
-            send(diff.at[yy * SIDE + xx], diffs.at[me], ds.at[k], dr.at[k], (yy * SIDE + xx, t))
-        )
-
     loads[10].wait()
     loads[11].wait()
     loads[12].wait()
@@ -445,6 +439,12 @@
         moved.append(send(mix.at[to], full.at[y, x, t], ts.at[k], tr.at[k], along_t(k)))
     full[y, x, t] = mix[some]
     uring.step(1, ALL)
+
+    for k, (i, j) in enumerate(plane):
+        yy, xx = (y + i) % SIDE, (x + j) % SIDE
+        others.append(
+            send(diff.at[yy * SIDE + xx], diffs.at[me], ds.at[k], dr.at[k], (yy * SIDE + xx, t))
+        )
     for copy in moved:
         copy.wait_recv()
     sweeps = [
@@ -524,33 +524,11 @@
     lax.fori_loop(0, 16, outer, 0)
     swapped = send(co.at[:, 1 - c], rc, s7.at[0], r7.at[0], other_core())
 
-    second_b = []
-    for part, (a, b) in enumerate(cuts):
-        for copy in first_b[6 * part : 6 * part + 6]:
-            copy.wait_recv()
-        for i in range(SIDE):
-            total = bp[a:b, y, i].astype(F32)
-            for j in range(3):
-                total = total + ra[j, a:b, i].astype(F32)
-            sa[i, a:b] = total.astype(BF)
-            total = bp[8 + a : 8 + b, i, x].astype(F32)
-            for j in range(3):
-                total = total + rb[j, a:b, i].astype(F32)
-            sb[i, a:b] = total.astype(BF)
-        here = pl.ds(a, b - a)
-        for j in NEAR:
-            src, sem = sa.at[(x + j) % SIDE, here], (part, 0, j - 1)
-            second_b.append(send(src, qa.at[j - 1, here], s2.at[sem], r2.at[sem], along_x(j)))
-            src, sem = sb.at[(y + j) % SIDE, here], (part, 1, j - 1)
-            second_b.append(send(src, qb.at[j - 1, here], s2.at[sem], r2.at[sem], along_y(j)))
-
-    swapped.wait_recv()
 
     def pair(k, _):
         sc[k] = (co[k, c].astype(F32) + rc[k].astype(F32)).astype(BF)
         return 0
 
-    lax.fori_loop(0, 8, pair, 0)
     shares = []
 
     def pass_on(step):
@@ -575,7 +553,31 @@
                 send(src, dst, s4.at[way, step], r4.at[way, step], along_z(sign))
             )
 
-    pass_on(0)
+
+    second_b = []
+    for part, (a, b) in enumerate(cuts):
+        for copy in first_b[6 * part : 6 * part + 6]:
+            copy.wait_recv()
+        for i in range(SIDE):
+            total = bp[a:b, y, i].astype(F32)
+            for j in range(3):
+                total = total + ra[j, a:b, i].astype(F32)
+            sa[i, a:b] = total.astype(BF)
+            total = bp[8 + a : 8 + b, i, x].astype(F32)
+            for j in range(3):
+                total = total + rb[j, a:b, i].astype(F32)
+            sb[i, a:b] = total.astype(BF)
+        here = pl.ds(a, b - a)
+        for j in NEAR:
+            src, sem = sa.at[(x + j) % SIDE, here], (part, 0, j - 1)
+            second_b.append(send(src, qa.at[j - 1, here], s2.at[sem], r2.at[sem], along_x(j)))
+            src, sem = sb.at[(y + j) % SIDE, here], (part, 1, j - 1)
+            second_b.append(send(src, qb.at[j - 1, here], s2.at[sem], r2.at[sem], along_y(j)))
+        if part == 0:
+            swapped.wait_recv()
+            lax.fori_loop(0, 8, pair, 0)
+            pass_on(0)
+    pass_on(1)
     for copy in second_b:
         copy.wait_recv()
     total = sa[x].astype(F32)
@@ -591,7 +593,7 @@
         third.append(send(done.at[(t + k) % 16], bt.at[t], s3.at[k], r3.at[k], along_t(k)))
     bt[t] = done[t]
 
-    pass_on(1)
+    pass_on(2)
     for copy in third:
         copy.wait_recv()
     back = bt[...].reshape(COUNT, WIDE).astype(F32).T.astype(BF)
@@ -603,7 +605,7 @@
             fourth.append(
                 send(vb.at[h], got.at[j - 1], s5.at[h, j - 1], r5.at[h, j - 1], along(j))
             )
-    pass_on(2)
+    pass_on(3)
     loads[13].wait()
     loads[14].wait()
     def inner(a1, b1, a2, b2):
@@ -639,7 +641,6 @@
                 fifth.append(
                     send(outb.at[k - 1], to.at[k - 1], s6.at[h, k - 1], r6.at[h, k - 1], along(k))
                 )
-    pass_on(3)
     for copy in fifth:
         copy.wait_recv()
     for h, (own, got) in enumerate(((cxf, hx), (cyf, hy))):

time: 147 us -> 147 us (level)
  no operation moved by 1% of the time
where the time goes in v8:
time: 147 us
  Pallas kernels  146 us (99%)
    pallas_call x1, Pallas kernels, body(): pl.pallas_call(step_kernel, out_shape=(jax.ShapeDtypeStruct((BLOCK, WIDE)...  144 us

profile of v8, /device:TPU:1, one launch (start us, length us, event | category | flops | bytes accessed | tf_op | source)
XLA Modules:
  0.0 147.1 jit_solution(14867339167091499310)
XLA Ops:
  1.3 143.8 %shard_map.148 = (f32[384,256]{1,0:T(8,128)}, f32[256,384]{1,0:T(8,128)}, f32[8,128]{1,0:T(8,128)}) custom-call(bf16[256,6144]{1,0:T(8,128)(2,1)} %tokens.1, bf16[256,6144]{1,0:T(8,128)(2,1)} %target.1, f32[256,2,256]{2,1,0:T(2,128)} %bias.1, s32[256,256]{1,0:T(8,128)} %near.1, bf16[384,256]{1,0:T(8,128)(2,1)} %wq.1, bf16[384,256]{1,0:T(8,128)(2,1)} %wk.1, ...), custom_call_target="tpu_custom_call" | custom-call | tf_op jit(solution)/shard_map/pallas_call | solution.py:804
  145.1 2.1 %shard_map.149 = (f32[384,256]{1,0:T(8,128)}, f32[256,384]{1,0:T(8,128)}, f32[2]{0:T(128)}) custom-call(f32[384,256]{1,0:T(8,128)} %get-tuple-element.6.rest_value, f32[256,384]{1,0:T(8,128)} %get-tuple-element.7.rest_out, f32[8,128]{1,0:T(8,128)} %get-tuple-element.8.coef), custom_call_target="tpu_custom_call" | custom-call | tf_op jit(solution)/shard_map/pallas_call | solution.py:832
